TPU v7x, 32 devices: a whole 2x2x4 slice. The times are simulated.
32 devices in a mesh: grid: 4 (over y, x), strip: 8 (over z, core).
Axes of the slice: x: 2, y: 2, z: 4, core: 2. Of those that a mesh axis runs over, the one named last changes fastest.
Arguments:
- features: bfloat16 [4, 96, 72, 128], P('grid', 'strip'), may hold values from -6 to 6
- cell_frame: int32 [4, 96, 72], P('grid', 'strip'), may hold values from 0 to 3, as said below
- cotangent: bfloat16 [4, 96, 72, 128], P('grid', 'strip'), may hold values from -12 to 12
- attend_weight: float32 [2, 128, 384], replicated, may hold values from -0.5 to 0.5
- output_weight: float32 [2, 128, 128], replicated, may hold values from -1.5 to 1.5
- expand_weight: float32 [2, 128, 256], replicated, may hold values from -0.5 to 0.5
- reduce_weight: float32 [2, 256, 128], replicated, may hold values from -0.375 to 0.375
- position_table: float32 [2, 144, 128], replicated, may hold values from -4 to 4
- norm_params: float32 [2, 4, 128], replicated, may hold values from -0.75 to 1.75, as said below
- attend_first: float32 [2, 128, 384], replicated, may hold values from -0.0029296875 to 0.0029296875
- output_first: float32 [2, 128, 128], replicated, may hold values from -0.0029296875 to 0.0029296875
- expand_first: float32 [2, 128, 256], replicated, may hold values from -0.0029296875 to 0.0029296875
- reduce_first: float32 [2, 256, 128], replicated, may hold values from -0.0029296875 to 0.0029296875
- position_first: float32 [2, 144, 128], replicated, may hold values from -0.00024414062 to 0.00024414062
- norms_first: float32 [2, 4, 128], replicated, may hold values from -0.0078125 to 0.0078125
- attend_second: float32 [2, 128, 384], replicated, may hold values from 3.332978e-09 to 1.3331912e-08
- output_second: float32 [2, 128, 128], replicated, may hold values from 3.332978e-09 to 1.3331912e-08
- expand_second: float32 [2, 128, 256], replicated, may hold values from 3.332978e-09 to 1.3331912e-08
- reduce_second: float32 [2, 256, 128], replicated, may hold values from 3.332978e-09 to 1.3331912e-08
- position_second: float32 [2, 144, 128], replicated, may hold values from 2.314568e-11 to 9.258272e-11
- norms_second: float32 [2, 4, 128], replicated, may hold values from 2.6663823e-08 to 1.0665529e-07
Outputs:
- block_output: bfloat16 [4, 96, 72, 128], P('grid', 'strip')
- input_grad: float32 [4, 96, 72, 128], P('grid', 'strip')
- attend_updated: float32 [2, 128, 384], replicated
- output_updated: float32 [2, 128, 128], replicated
- expand_updated: float32 [2, 128, 256], replicated
- reduce_updated: float32 [2, 256, 128], replicated
- position_updated: float32 [2, 144, 128], replicated
- norms_updated: float32 [2, 4, 128], replicated
- attend_moment: float32 [2, 128, 384], replicated
- output_moment: float32 [2, 128, 128], replicated
- expand_moment: float32 [2, 128, 256], replicated
- reduce_moment: float32 [2, 256, 128], replicated
- position_moment: float32 [2, 144, 128], replicated
- norms_moment: float32 [2, 4, 128], replicated
- attend_squares: float32 [2, 128, 384], replicated
- output_squares: float32 [2, 128, 128], replicated
- expand_squares: float32 [2, 128, 256], replicated
- reduce_squares: float32 [2, 256, 128], replicated
- position_squares: float32 [2, 144, 128], replicated
- norms_squares: float32 [2, 4, 128], replicated
- clip_norm: float32 [], replicated
- tensor_norms: float32 [2, 9, 2], replicated
Inputs may be any that keep to these rules, and one draw needn't show every extreme that they name: `cell_frame`: 0 marks an empty cell; the frames 1 to 3 are bands of whole columns over all 96 rows of a grid. `norm_params`: rows 0 and 2 of each layer are gains near one, rows 1 and 3 biases near zero.
All inputs are finite; a program needn't handle non-finite values.
Results may differ from a plain program's by a relative error of at most 0.02.
The roundings to bfloat16 on the way count: a program that leaves them out, or rounds other values in their place, can miss the bound.
Values may be sent and summed in bfloat16 or wider, within the bound.
A program may use at most 128 MiB of HBM per device.

v0:
```python
import functools

import jax
import jax.numpy as jnp
import numpy as np
from jax import lax
from jax.experimental import pallas as pl
from jax.experimental.pallas import tpu as pltpu
from jax.sharding import PartitionSpec as P

bf16 = jnp.bfloat16
f32 = jnp.float32
MESH = pl.DeviceIdType.MESH

HEADS = 8
HEAD = 16
D = 128
FF = 256
WIN = 12
SLOTS = WIN * WIN
LANES = HEADS * SLOTS
STEP = 10
beta_one = 0.9
beta_two = 0.999
learn_rate = 0.2
weight_decay = 0.01
epsilon = 1e-06
clip_bound = 1.0

Q0, K0, V0, O0, E0, R0, P0, N0 = 0, 128, 256, 384, 512, 768, 1024, 1168
ROWS = 1176
TOTAL = 2432

TILES = ((0, 256), (256, 512), (512, 768), (768, 1024), (1024, 1152))


def nt(a, b):
    return lax.dot_general(a, b, (((1,), (1,)), ((), ())), preferred_element_type=f32)


def tn(a, b):
    return lax.dot_general(a, b, (((0,), (0,)), ((), ())), preferred_element_type=f32)


def nn(a, b):
    return jnp.dot(a, b, preferred_element_type=f32)


def head_blocks(block):
    lane = lax.broadcasted_iota(jnp.int32, block.shape, 1)
    parts = []
    for h in range(HEADS):
        keep = (lane >= h * HEAD) & (lane < (h + 1) * HEAD)
        parts.append(jnp.where(keep, block, jnp.zeros_like(block)))
    return jnp.concatenate(parts, axis=0)


def diagonal(full):
    return jnp.concatenate(
        [full[h * HEAD : (h + 1) * HEAD, h * SLOTS : (h + 1) * SLOTS] for h in range(HEADS)], axis=0
    )


def main_kernel(
    strips,
    windows,
    feat,
    codes_in,
    cot,
    attend_w,
    output_w,
    expand_w,
    reduce_w,
    position,
    norms,
    block_out,
    input_grad,
    grads_out,
    wa,
    wo,
    we,
    wr,
    xt,
    mi,
    qs,
    ks,
    vs,
    probs,
    att,
    first_b,
    xh1,
    rs1,
    act,
    dgelu,
    xh2,
    rs2,
    crow,
    ccol,
    ctab,
    field,
    wide,
    tmp,
    d_br2,
    d_hid,
    d_br,
    d_att,
    d_res,
    ds_s,
    d_q,
    d_k,
    d_v,
    csend,
    crecv,
    hsend,
    hrecv,
    osend,
    orecv,
    grecv,
    bsend,
    brecv,
    g,
    s1,
    r1,
    hsum,
    s2,
    r2,
    s3,
    r3,
    half_b,
    all_b,
    send_sem,
    recv_sem,
):
    T = windows * SLOTS
    cols = windows * WIN
    stride = cols + 8
    hw = WIN // 2
    hs = hw * WIN
    gi = lax.axis_index("grid")
    si = lax.axis_index("strip")
    n_grid = lax.axis_size("grid")
    core = lax.rem(si, 2)
    zi = lax.div(si, 2)
    n_z = strips // 2
    prev = lax.rem(si + strips - 1, strips)
    nxt = lax.rem(si + 1, strips)
    sib = si + 1 - 2 * core

    grid_peers = [lax.rem(gi + d, n_grid) for d in range(1, n_grid)]
    z_peers = [lax.rem(zi + d, n_z) * 2 + core for d in range(1, n_z)]
    peers = [(gi, prev), (gi, nxt), (gi, sib)]
    peers += [(p, si) for p in grid_peers] + [(gi, p) for p in z_peers]

    barrier = pltpu.get_barrier_semaphore()
    for peer in peers:
        pl.semaphore_signal(barrier, inc=1, device_id=peer, device_id_type=MESH)
    pl.semaphore_wait(barrier, len(peers))

    def remote(src, dst, index, device):
        return pltpu.make_async_remote_copy(
            src_ref=src,
            dst_ref=dst,
            send_sem=send_sem.at[index],
            recv_sem=recv_sem.at[index],
            device_id=device,
            device_id_type=MESH,
        )

    csend[...] = jnp.zeros((16, 128), f32)
    csend[0:WIN, 0:cols] = codes_in[...].astype(f32)
    codes_copy = remote(csend, crecv, 0, (gi, prev))
    codes_copy.start()
    cot_copy = remote(cot.at[pl.ds(0, hw)], grecv, 1, (gi, prev))
    cot_copy.start()

    for l in range(2):
        wa[l] = attend_w[l].astype(bf16)
        wo[l] = output_w[l].astype(bf16)
        we[l] = expand_w[l].astype(bf16)
        wr[l] = reduce_w[l].astype(bf16)

    def code_tables(l, table):
        low = table.astype(bf16)
        lane = lax.broadcasted_iota(jnp.int32, (16, LANES), 1).astype(f32)
        row = lax.broadcasted_iota(jnp.int32, (16, LANES), 0).astype(f32)
        slot = lane - SLOTS * jnp.floor((lane + 0.5) * (1.0 / SLOTS))
        slot_r = jnp.floor((slot + 0.5) * (1.0 / WIN))
        slot_c = slot - WIN * slot_r
        pick_r = (slot_r == row).astype(bf16)
        ctab[...] = tn(low, pick_r)
        pick_c = (slot_c == row).astype(f32)[0:WIN]
        for w in range(windows):
            part = ctab[w * WIN : (w + 1) * WIN, :]
            crow[l, w] = jnp.sum(part * pick_c, axis=0, keepdims=True)
        token = lax.broadcasted_iota(jnp.int32, (SLOTS, 128), 0).astype(f32)
        place = lax.broadcasted_iota(jnp.int32, (SLOTS, 128), 1).astype(f32)
        token_r = jnp.floor((token + 0.5) * (1.0 / WIN))
        token_c = token - WIN * token_r
        row_of = (token_r == place).astype(bf16)[:, 0:16]
        spread = nn(row_of, low)
        for w in range(windows):
            chosen = jnp.where(place == token_c + w * WIN, spread, 0.0)
            value = jnp.sum(chosen, axis=1, keepdims=True)
            ccol[l, w * SLOTS : (w + 1) * SLOTS] = jnp.broadcast_to(value, (SLOTS, 128))

    code_tables(0, csend[...])

    def attention_forward(l):
        def one(w, carry):
            off = pl.multiple_of(w * SLOTS, SLOTS)
            rows = pl.ds(off, SLOTS)
            q = qs[l, rows]
            k = ks[l, rows]
            v_t = vs[l, rows].T
            qb = head_blocks(q)
            cc = ccol[l, rows]
            cr = crow[l, w]
            for a, b in TILES:
                scores = nt(k, qb[a:b])
                same = jnp.concatenate([cc] * ((b - a) // 128), axis=1) == cr[:, a:b]
                scores = jnp.where(same, scores, -1000000000.0)
                top = jnp.max(scores, axis=0, keepdims=True)
                weights = jnp.exp(scores - top)
                total = jnp.sum(weights, axis=0, keepdims=True)
                p = (weights * (1.0 / total)).astype(bf16)
                probs[l, rows, a:b] = p
                tmp[:, a:b] = nn(v_t, p)
            att[l, rows] = diagonal(tmp[...]).T.astype(bf16)
            return carry

        lax.fori_loop(0, windows, one, 0)

    def layer_forward(l, finish):
        def first_part(w, carry):
            rows = pl.ds(pl.multiple_of(w * SLOTS, SLOTS), SLOTS)
            x = xt[l, rows]
            m = (x.astype(f32) + position[l]).astype(bf16)
            mi[l, rows] = m
            qk = nn(m, wa[l, :, 0 : 2 * D])
            qs[l, rows] = (qk[:, 0:D] * HEAD ** (-0.5)).astype(bf16)
            ks[l, rows] = qk[:, D : 2 * D].astype(bf16)
            vs[l, rows] = nn(x, wa[l, :, 2 * D : 3 * D]).astype(bf16)
            return carry

        lax.fori_loop(0, windows, first_part, 0)
        attention_forward(l)

        def second_part(w, carry):
            rows = pl.ds(pl.multiple_of(w * SLOTS, SLOTS), SLOTS)
            r = xt[l, rows].astype(f32) + nn(att[l, rows], wo[l])
            c = r - jnp.mean(r, axis=1, keepdims=True)
            s = lax.rsqrt(jnp.mean(c * c, axis=1, keepdims=True) + 1e-05)
            n = c * s
            xh1[l, rows] = n
            rs1[l, rows] = jnp.broadcast_to(s, (SLOTS, D))
            first = n * norms[l, 0:1] + norms[l, 1:2]
            fb = first.astype(bf16)
            first_b[l, rows] = fb
            h = nn(fb, we[l])
            h2 = h * h
            t = jnp.tanh(0.7978845608028654 * h * (1.0 + 0.044715 * h2))
            act_b = (0.5 * h * (1.0 + t)).astype(bf16)
            act[l, rows] = act_b
            dgelu[l, rows] = 0.5 * (1.0 + t) + 0.5 * h * (1.0 - t * t) * (
                0.7978845608028654 * (1.0 + 3.0 * 0.044715 * h2)
            )
            r = first + nn(act_b, wr[l])
            c = r - jnp.mean(r, axis=1, keepdims=True)
            s = lax.rsqrt(jnp.mean(c * c, axis=1, keepdims=True) + 1e-05)
            n = c * s
            xh2[l, rows] = n
            rs2[l, rows] = jnp.broadcast_to(s, (SLOTS, D))
            second = n * norms[l, 2:3] + norms[l, 3:4]
            second = jnp.where(ccol[l, rows] > 0.0, second, 0.0)
            wide[rows] = second.astype(bf16).astype(f32)
            return carry

        lax.fori_loop(0, windows, second_part, 0)

    def norm_back(d, gain, n, s):
        dn = d * gain
        m1 = jnp.mean(dn, axis=1, keepdims=True)
        m2 = jnp.mean(dn * n, axis=1, keepdims=True)
        return s * (dn - m1 - n * m2)

    def layer_backward(l):
        base = l * ROWS
        zero = jnp.zeros((1, D), f32)

        def dense(w, sums):
            rows = pl.ds(pl.multiple_of(w * SLOTS, SLOTS), SLOTS)
            d = jnp.where(ccol[l, rows] > 0.0, wide[rows], 0.0)
            n2 = xh2[l, rows]
            bias2 = jnp.sum(d, axis=0, keepdims=True)
            gain2 = jnp.sum(d * n2, axis=0, keepdims=True)
            d2 = norm_back(d, norms[l, 2:3], n2, rs2[l, rows])
            b2 = d2.astype(bf16)
            d_br2[rows] = b2
            dh = (nt(b2, wr[l]) * dgelu[l, rows]).astype(bf16)
            d_hid[rows] = dh
            d1 = d2 + nt(dh, we[l])
            n1 = xh1[l, rows]
            bias1 = jnp.sum(d1, axis=0, keepdims=True)
            gain1 = jnp.sum(d1 * n1, axis=0, keepdims=True)
            dr = norm_back(d1, norms[l, 0:1], n1, rs1[l, rows])
            d_res[rows] = dr
            b1 = dr.astype(bf16)
            d_br[rows] = b1
            d_att[rows] = nt(b1, wo[l]).astype(bf16)
            return tuple(a + b for a, b in zip(sums, (gain1, bias1, gain2, bias2)))

        sums = lax.fori_loop(0, windows, dense, (zero,) * 4)
        g[base + N0 : base + N0 + 8] = jnp.concatenate(list(sums) + [jnp.zeros((4, D), f32)], axis=0)
        g[base + R0 : base + R0 + FF] = tn(act[l], d_br2[...])
        d_expand = tn(first_b[l], d_hid[...])
        g[base + E0 : base + E0 + D] = d_expand[:, 0:D]
        g[base + E0 + D : base + E0 + 2 * D] = d_expand[:, D : 2 * D]
        g[base + O0 : base + O0 + D] = tn(att[l], d_br[...])

        def one(w, carry):
            rows = pl.ds(pl.multiple_of(w * SLOTS, SLOTS), SLOTS)
            v = vs[l, rows]
            k_t = ks[l, rows].T
            qb = head_blocks(qs[l, rows])
            db = head_blocks(d_att[rows])
            for a, b in TILES:
                dp = nt(v, db[a:b])
                p = probs[l, rows, a:b].astype(f32)
                ds = p * (dp - jnp.sum(dp * p, axis=0, keepdims=True))
                ds = ds.astype(bf16)
                ds_s[:, a:b] = ds
                tmp[:, a:b] = nn(k_t, ds)
            d_v[rows] = nn(probs[l, rows], db).astype(bf16)
            d_k[rows] = nn(ds_s[...], qb).astype(bf16)
            d_q[rows] = (diagonal(tmp[...]).T * HEAD ** (-0.5)).astype(bf16)
            return carry

        lax.fori_loop(0, windows, one, 0)
        g[base + Q0 : base + Q0 + D] = tn(mi[l], d_q[...])
        g[base + K0 : base + K0 + D] = tn(mi[l], d_k[...])
        g[base + V0 : base + V0 + D] = tn(xt[l], d_v[...])

        def last(w, d_pos):
            rows = pl.ds(pl.multiple_of(w * SLOTS, SLOTS), SLOTS)
            dm = nt(d_q[rows], wa[l, :, 0:D]) + nt(d_k[rows], wa[l, :, D : 2 * D])
            wide[rows] = d_res[rows] + dm + nt(d_v[rows], wa[l, :, 2 * D : 3 * D])
            return d_pos + dm

        d_pos = lax.fori_loop(0, windows, last, jnp.zeros((SLOTS, D), f32))
        g[base + P0 : base + P0 + SLOTS] = d_pos

    for r in range(WIN):
        field[r * stride : r * stride + cols] = feat[r].astype(f32)
    for w in range(windows):
        for r in range(WIN):
            a = w * SLOTS + r * WIN
            wide[a : a + WIN] = field[r * stride + w * WIN : r * stride + (w + 1) * WIN]
    xt[0] = wide[...].astype(bf16)
    layer_forward(0, None)

    for w in range(windows):
        hsend[w * hs : (w + 1) * hs] = wide[w * SLOTS : w * SLOTS + hs].astype(bf16)
    halo_copy = remote(hsend, hrecv, 2, (gi, prev))
    halo_copy.start()
    codes_copy.wait()
    own = csend[...]
    other = crecv[...]
    table = jnp.concatenate([own[hw:WIN], other[0:hw], jnp.zeros((4, 128), f32)], axis=0)
    table = jnp.concatenate(
        [table[:, hw:cols], table[:, 0:hw], jnp.zeros((16, 128 - cols), f32)], axis=1
    )
    code_tables(1, table)

    def to_shifted():
        for w in range(windows):
            for r in range(WIN):
                a = w * SLOTS + r * WIN
                b = r * stride + w * WIN + hw
                wide[a : a + WIN] = field[b : b + WIN]

    for w in range(windows):
        for r in range(hw):
            a = w * SLOTS + (r + hw) * WIN
            field[r * stride + w * WIN : r * stride + (w + 1) * WIN] = wide[a : a + WIN]
    halo_copy.wait()
    wide[0 : windows * hs] = hrecv[...].astype(f32)
    for w in range(windows):
        for r in range(hw):
            a = w * hs + r * WIN
            b = (r + hw) * stride
            field[b + w * WIN : b + (w + 1) * WIN] = wide[a : a + WIN]
    for r in range(WIN):
        field[r * stride + cols : r * stride + cols + hw] = field[r * stride : r * stride + hw]
    to_shifted()
    xt[1] = wide[...].astype(bf16)
    layer_forward(1, None)

    for w in range(windows):
        osend[w * hs : (w + 1) * hs] = wide[w * SLOTS + hs : (w + 1) * SLOTS].astype(bf16)
    out_copy = remote(osend, orecv, 3, (gi, nxt))
    out_copy.start()

    def from_shifted(source, source_rows, first_row):
        for w in range(windows):
            for r in range(hw):
                a = w * source_rows + r * WIN
                b = (r + first_row) * stride + w * WIN + hw
                field[b : b + WIN] = source[a : a + WIN]
        for r in range(first_row, first_row + hw):
            field[r * stride : r * stride + hw] = field[r * stride + cols : r * stride + cols + hw]

    from_shifted(wide, SLOTS, hw)
    for r in range(hw, WIN):
        block_out[r] = field[r * stride : r * stride + cols].astype(bf16)

    cot_copy.wait()
    for r in range(hw):
        field[r * stride : r * stride + cols] = cot[r + hw].astype(f32)
        field[(r + hw) * stride : (r + hw) * stride + cols] = grecv[r].astype(f32)
    for r in range(WIN):
        field[r * stride + cols : r * stride + cols + hw] = field[r * stride : r * stride + hw]
    to_shifted()
    layer_backward(1)

    for w in range(windows):
        bsend[w * hs : (w + 1) * hs] = wide[w * SLOTS + hs : (w + 1) * SLOTS].astype(bf16)
    back_copy = remote(bsend, brecv, 4, (gi, nxt))
    back_copy.start()
    from_shifted(wide, SLOTS, hw)
    back_copy.wait()
    wide[0 : windows * hs] = brecv[...].astype(f32)
    from_shifted(wide, hs, 0)
    for w in range(windows):
        for r in range(WIN):
            a = w * SLOTS + r * WIN
            wide[a : a + WIN] = field[r * stride + w * WIN : r * stride + (w + 1) * WIN]
    wide[...] = wide[...].astype(bf16).astype(f32)
    layer_backward(0)
    for w in range(windows):
        for r in range(WIN):
            a = w * SLOTS + r * WIN
            field[r * stride + w * WIN : r * stride + (w + 1) * WIN] = wide[a : a + WIN]
    for r in range(WIN):
        input_grad[r] = field[r * stride : r * stride + cols]
    out_copy.wait()
    wide[0 : windows * hs] = orecv[...].astype(f32)
    from_shifted(wide, hs, 0)
    for r in range(hw):
        block_out[r] = field[r * stride : r * stride + cols].astype(bf16)

    half = TOTAL // 2
    quarter = half // n_grid
    g[2 * ROWS : TOTAL] = jnp.zeros((TOTAL - 2 * ROWS, D), f32)
    s1[...] = g[pl.ds(pl.multiple_of((1 - core) * half, 16), half)].astype(bf16)
    copy = remote(s1, r1, 5, (gi, sib))
    copy.start()
    copy.wait()
    hsum[...] = g[pl.ds(pl.multiple_of(core * half, 16), half)] + r1[...].astype(f32)
    s2[...] = hsum[...].astype(bf16)
    index = 6
    copies = []
    for d, p in enumerate(grid_peers):
        part = pl.ds(pl.multiple_of(p * quarter, 16), quarter)
        copies.append(remote(s2.at[part], r2.at[d], index, (p, si)))
        copies[-1].start()
        index += 1
    for copy in copies:
        copy.wait()
    mine = pl.ds(pl.multiple_of(gi * quarter, 16), quarter)
    total = hsum[mine]
    for d in range(n_grid - 1):
        total = total + r2[d].astype(f32)
    s3[...] = total.astype(bf16)
    copies = []
    for p in z_peers:
        copies.append(remote(s3, r3.at[zi], index, (gi, p)))
        copies[-1].start()
        index += 1
    r3[zi] = s3[...]
    for copy in copies:
        copy.wait()
    total = r3[0].astype(f32)
    for d in range(1, n_z):
        total = total + r3[d].astype(f32)
    half_b[mine] = total.astype(bf16)
    copies = []
    for p in grid_peers:
        copies.append(remote(half_b.at[mine], half_b.at[mine], index, (p, si)))
        copies[-1].start()
        index += 1
    for copy in copies:
        copy.wait()
    own_half = pl.ds(pl.multiple_of(core * half, 16), half)
    copy = remote(half_b, all_b.at[own_half], index, (gi, sib))
    copy.start()
    all_b[own_half] = half_b[...]
    copy.wait()
    grads_out[...] = all_b[...].astype(f32)


def main_call(strips, windows, cols, n_grid):
    T = windows * SLOTS
    hw = WIN // 2
    half = TOTAL // 2
    quarter = half // n_grid
    n_z = strips // 2
    vm = pltpu.VMEM
    hs = windows * hw * WIN
    copies = 5 + 1 + 2 * (n_grid - 1) + (n_z - 1) + 1
    scratch = [
        vm((2, D, 3 * D), bf16),
        vm((2, D, D), bf16),
        vm((2, D, FF), bf16),
        vm((2, FF, D), bf16),
        vm((2, T, D), bf16),
        vm((2, T, D), bf16),
        vm((2, T, D), bf16),
        vm((2, T, D), bf16),
        vm((2, T, D), bf16),
        vm((2, T, LANES), bf16),
        vm((2, T, D), bf16),
        vm((2, T, D), bf16),
        vm((2, T, D), f32),
        vm((2, T, D), f32),
        vm((2, T, FF), bf16),
        vm((2, T, FF), f32),
        vm((2, T, D), f32),
        vm((2, T, D), f32),
        vm((2, windows, 1, LANES), f32),
        vm((2, T, D), f32),
        vm((128, LANES), f32),
        vm((WIN * (cols + 8), D), f32),
        vm((T, D), f32),
        vm((D, LANES), f32),
        vm((T, D), bf16),
        vm((T, FF), bf16),
        vm((T, D), bf16),
        vm((T, D), bf16),
        vm((T, D), f32),
        vm((SLOTS, LANES), bf16),
        vm((T, D), bf16),
        vm((T, D), bf16),
        vm((T, D), bf16),
        vm((16, 128), f32),
        vm((16, 128), f32),
        vm((hs, D), bf16),
        vm((hs, D), bf16),
        vm((hs, D), bf16),
        vm((hs, D), bf16),
        vm((hw, cols, D), bf16),
        vm((hs, D), bf16),
        vm((hs, D), bf16),
        vm((TOTAL, D), f32),
        vm((half, D), bf16),
        vm((half, D), bf16),
        vm((half, D), f32),
        vm((half, D), bf16),
        vm((n_grid - 1, quarter, D), bf16),
        vm((quarter, D), bf16),
        vm((n_z, quarter, D), bf16),
        vm((half, D), bf16),
        vm((TOTAL, D), bf16),
        pltpu.SemaphoreType.DMA((copies,)),
        pltpu.SemaphoreType.DMA((copies,)),
    ]
    whole = pl.BlockSpec(memory_space=pltpu.VMEM)
    return pl.pallas_call(
        functools.partial(main_kernel, strips, windows),
        out_shape=(
            jax.ShapeDtypeStruct((WIN, cols, D), bf16),
            jax.ShapeDtypeStruct((WIN, cols, D), f32),
            jax.ShapeDtypeStruct((TOTAL, D), f32),
        ),
        in_specs=[whole] * 9,
        out_specs=(whole,) * 3,
        scratch_shapes=scratch,
        compiler_params=pltpu.CompilerParams(
            collective_id=0, has_side_effects=True, vmem_limit_bytes=56 * 1024 * 1024
        ),
    )


def lamb_kernel(*refs):
    grads, block_in, input_in = refs[0:3]
    weights = refs[3:9]
    firsts = refs[9:15]
    seconds = refs[15:21]
    block_out, input_out = refs[21:23]
    updated = refs[23:29]
    moments = refs[29:35]
    squares = refs[35:41]
    clip_out, norms_out = refs[41:43]
    sems = refs[43]
    moves = [
        pltpu.make_async_copy(block_in, block_out, sems.at[0]),
        pltpu.make_async_copy(input_in, input_out, sems.at[1]),
    ]
    for move in moves:
        move.start()
    every = grads[...]
    clip_norm = jnp.sqrt(jnp.sum(every * every, keepdims=True))
    clip_out[...] = clip_norm
    factor = clip_bound / jnp.maximum(clip_norm, clip_bound)
    fix_one = 1.0 / (1.0 - beta_one**STEP)
    fix_two = 1.0 / (1.0 - beta_two**STEP)

    def step(index, where, grad, decay):
        grad = grad * factor
        old = weights[index][where]
        moment = beta_one * firsts[index][where] + (1.0 - beta_one) * grad
        square = beta_two * seconds[index][where] + (1.0 - beta_two) * grad * grad
        moments[index][where] = moment
        squares[index][where] = square
        direction = moment * fix_one / (jnp.sqrt(square * fix_two) + epsilon)
        if decay:
            direction = direction + weight_decay * old
        return old, direction

    for l in range(2):
        base = l * ROWS
        found = []
        for index, first_row, blocks, height in (
            (0, Q0, 3, D),
            (1, O0, 1, D),
            (2, E0, 2, D),
            (3, R0, 1, FF),
            (4, P0, 1, SLOTS),
        ):
            parts = []
            for b in range(blocks):
                where = (l, slice(None), slice(b * D, (b + 1) * D))
                start = base + first_row + b * height
                parts.append((where,) + step(index, where, grads[start : start + height], True))
            weight_norm = jnp.sqrt(sum(jnp.sum(old * old, keepdims=True) for _, old, _ in parts))
            step_norm = jnp.sqrt(sum(jnp.sum(d * d, keepdims=True) for _, _, d in parts))
            scale = learn_rate * weight_norm / (step_norm + epsilon)
            for where, old, direction in parts:
                updated[index][where] = old - scale * direction
            found.append((weight_norm, step_norm))
        old, direction = step(5, (l,), grads[base + N0 : base + N0 + 4], False)
        weight_norm = jnp.sqrt(jnp.sum(old * old, axis=1, keepdims=True))
        step_norm = jnp.sqrt(jnp.sum(direction * direction, axis=1, keepdims=True))
        updated[5][l] = old - learn_rate * weight_norm / (step_norm + epsilon) * direction
        for r in range(4):
            found.append((weight_norm[r : r + 1], step_norm[r : r + 1]))
        row = lax.broadcasted_iota(jnp.int32, (9, 2), 0)
        lane = lax.broadcasted_iota(jnp.int32, (9, 2), 1)
        table = jnp.zeros((9, 2), f32)
        for t, pair in enumerate(found):
            for j in range(2):
                value = jnp.broadcast_to(pair[j], (9, 2))
                table = jnp.where((row == t) & (lane == j), value, table)
        norms_out[l] = table
    for move in moves:
        move.wait()


def lamb_call(grads, block_output, input_grad, weights, firsts, seconds):
    whole = pl.BlockSpec(memory_space=pltpu.VMEM)
    far = pl.BlockSpec(memory_space=pl.ANY)
    like = lambda a: jax.ShapeDtypeStruct(a.shape, a.dtype)
    out = [like(block_output), like(input_grad)]
    out += [like(a) for a in weights] * 3
    out += [jax.ShapeDtypeStruct((1, 1), f32), jax.ShapeDtypeStruct((2, 9, 2), f32)]
    return pl.pallas_call(
        lamb_kernel,
        out_shape=out,
        in_specs=[whole, far, far] + [whole] * 18,
        out_specs=[far, far] + [whole] * 20,
        scratch_shapes=[pltpu.SemaphoreType.DMA((2,))],
        compiler_params=pltpu.CompilerParams(vmem_limit_bytes=48 * 1024 * 1024),
    )(grads, block_output, input_grad, *weights, *firsts, *seconds)


def body(mesh, features, cell_frame, cotangent, *rest):
    weights, firsts, seconds = rest[0:6], rest[6:12], rest[12:18]
    cols = features.shape[2]
    call = main_call(mesh.shape["strip"], cols // WIN, cols, mesh.shape["grid"])
    block_output, input_grad, grads = call(features[0], cell_frame[0], cotangent[0], *weights)
    out = lamb_call(grads, block_output, input_grad, weights, firsts, seconds)
    return (out[0][None], out[1][None], *out[2:20], out[20].reshape(()), out[21])


def solution(mesh):
    cells = P("grid", "strip", None, None)
    return jax.shard_map(
        functools.partial(body, mesh),
        mesh=mesh,
        in_specs=(cells, P("grid", "strip", None), cells) + (P(),) * 18,
        out_specs=(cells, cells) + (P(),) * 20,
        check_vma=False,
    )
```

profile of v0, /device:TPU:0, one launch (start us, length us, event | category | flops | bytes accessed | tf_op | source)
XLA Modules:
  0.0 100.9 jit_solution(3527905730871369543)
XLA Ops:
  0.7 0.0 copy-start.18
  0.7 0.0 copy-start.4
  0.7 0.0 copy-start.3
  0.7 0.0 copy-start.2
  0.7 0.0 copy-start.5
  0.7 0.0 copy-start
  0.7 0.0 copy-start.20
  0.7 0.0 copy-start.19
  0.8 1.4 %copy.46 = s32[1,12,72]{2,1,0:T(8,128)} copy(s32[1,12,72]{2,0,1:T(1,128)} %param.22) | data formatting | bytes 6912
  2.2 81.9 %shard_map.372 = (bf16[12,72,128]{2,1,0:T(8,128)(2,1)}, f32[12,72,128]{2,1,0:T(8,128)}, f32[2432,128]{1,0:T(8,128)}) custom-call(bf16[12,72,128]{2,1,0:T(8,128)(2,1)} %bitcast.8, s32[12,72]{1,0:T(8,128)} %bitcast.10, bf16[12,72,128]{2,1,0:T(8,128)(2,1)} %bitcast.9, f32[2,128,384]{2,1,0:T(8,128)} %refs_3_.1, f32[2,128,128]{2,1,0:T(8,128)} %refs_4_.1, ...), custom_call_target="tpu_custom_call" | custom-call | tf_op jit(solution)/shard_map/pallas_call | solution.py:679
  84.2 1.3 %copy-done.1 = f32[2432,128]{1,0:T(8,128)S(1)} copy-done((f32[2432,128]{1,0:T(8,128)S(1)}, f32[2432,128]{1,0:T(8,128)}, u32[]{:S(2)}) %copy-start.1) | copy-done | bytes 1245208
  85.5 1.0 %copy-done.6 = f32[12,72,128]{2,1,0:T(8,128)S(1)} copy-done((f32[12,72,128]{2,1,0:T(8,128)S(1)}, f32[12,72,128]{2,1,0:T(8,128)}, u32[]{:S(2)}) %copy-start.6) | copy-done | bytes 442392
  86.5 1.0 copy-done.8
  87.5 0.9 copy-done.9
  88.4 0.9 copy-done.10
  89.4 0.9 copy-done.11
  90.3 0.9 copy-done.12
  91.3 0.9 copy-done.13
  92.2 0.9 copy-done.14
  93.1 0.9 copy-done.15
  94.0 0.9 copy-done.16
  94.9 0.9 copy-done.17
  95.8 4.4 %shard_map.373 = (bf16[12,72,128]{2,1,0:T(8,128)(2,1)}, f32[12,72,128]{2,1,0:T(8,128)}, f32[2,128,384]{2,1,0:T(8,128)}, f32[2,128,128]{2,1,0:T(8,128)}, f32[2,12...) custom-call(f32[2432,128]{1,0:T(8,128)S(1)} %copy-done.1, ...), custom_call_target="tpu_custom_call" | custom-call | tf_op jit(solution)/shard_map/pallas_call | solution.py:665
  100.3 0.7 copy.43
  (22 shorter events, 0.0 us)
Async XLA Ops:
  0.7 83.4 %copy-start.18 = (f32[2,4,128]{2,1,0:T(4,128)S(1)}, f32[2,4,128]{2,1,0:T(4,128)}, u32[]{:S(2)}) copy-start(f32[2,4,128]{2,1,0:T(4,128)} %refs_8_.1) | copy-start | bytes 12292
  0.7 83.4 %copy-start.4 = (f32[2,144,128]{2,1,0:T(8,128)S(1)}, f32[2,144,128]{2,1,0:T(8,128)}, u32[]{:S(2)}) copy-start(f32[2,144,128]{2,1,0:T(8,128)} %refs_7_.1) | copy-start | bytes 442372
  0.7 83.4 %copy-start.3 = (f32[2,256,128]{2,1,0:T(8,128)S(1)}, f32[2,256,128]{2,1,0:T(8,128)}, u32[]{:S(2)}) copy-start(f32[2,256,128]{2,1,0:T(8,128)} %refs_6_.1) | copy-start | bytes 786436
  0.7 83.4 %copy-start.2 = (f32[2,128,256]{2,1,0:T(8,128)S(1)}, f32[2,128,256]{2,1,0:T(8,128)}, u32[]{:S(2)}) copy-start(f32[2,128,256]{2,1,0:T(8,128)} %refs_5_.1) | copy-start | bytes 786436
  0.7 83.4 %copy-start.5 = (f32[2,128,128]{2,1,0:T(8,128)S(1)}, f32[2,128,128]{2,1,0:T(8,128)}, u32[]{:S(2)}) copy-start(f32[2,128,128]{2,1,0:T(8,128)} %refs_4_.1) | copy-start | bytes 393220
  0.7 83.4 %copy-start = (f32[2,128,384]{2,1,0:T(8,128)S(1)}, f32[2,128,384]{2,1,0:T(8,128)}, u32[]{:S(2)}) copy-start(f32[2,128,384]{2,1,0:T(8,128)} %refs_3_.1) | copy-start | bytes 1179652
  0.7 83.4 %copy-start.20 = (f32[2,4,128]{2,1,0:T(4,128)S(1)}, f32[2,4,128]{2,1,0:T(4,128)}, u32[]{:S(2)}) copy-start(f32[2,4,128]{2,1,0:T(4,128)} %refs_20_.1) | copy-start | bytes 12292
  0.7 83.4 %copy-start.19 = (f32[2,4,128]{2,1,0:T(4,128)S(1)}, f32[2,4,128]{2,1,0:T(4,128)}, u32[]{:S(2)}) copy-start(f32[2,4,128]{2,1,0:T(4,128)} %refs_14_.1) | copy-start | bytes 12292
  0.8 83.4 %copy-start.7 = (f32[2,128,384]{2,1,0:T(8,128)S(1)}, f32[2,128,384]{2,1,0:T(8,128)}, u32[]{:S(2)}) copy-start(f32[2,128,384]{2,1,0:T(8,128)} %refs_9_.1) | copy-start | bytes 1179652
  84.2 1.3 %copy-start.1 = (f32[2432,128]{1,0:T(8,128)S(1)}, f32[2432,128]{1,0:T(8,128)}, u32[]{:S(2)}) copy-start(f32[2432,128]{1,0:T(8,128)} %get-tuple-element.47.refs_0_) | copy-start | bytes 3735556
  85.5 1.0 %copy-start.6 = (f32[12,72,128]{2,1,0:T(8,128)S(1)}, f32[12,72,128]{2,1,0:T(8,128)}, u32[]{:S(2)}) copy-start(f32[12,72,128]{2,1,0:T(8,128)} %get-tuple-element.49.refs_2_) | copy-start | bytes 1327108
  86.5 1.0 copy-start.8
  87.5 0.9 copy-start.9
  88.4 0.9 copy-start.10
  89.4 0.9 copy-start.11
  90.3 0.9 copy-start.12
  91.3 0.9 copy-start.13
  92.2 0.9 copy-start.14
  93.1 0.9 copy-start.15
  94.0 0.9 copy-start.16
  94.9 0.9 copy-start.17
where the time goes:
time: 101 us
  Pallas kernels  86.3 us (85%)
  local copies, waits for them, and re-layouts  13.8 us (14%)
    pallas_call x1, Pallas kernels, body(): call(features[0], cell_frame[0], cotangent[0], *weights)  81.9 us
    unnamed x44, local copies, waits for them, and re-layouts  13.8 us
    pallas_call x1, Pallas kernels, lamb_call(): pl.pallas_call(lamb_kernel, out_shape=out, in_specs=[whole, far, far] + [...  4.42 us

commit v1 on v0

v1 whole, which is shorter than its diff:
```python
import functools

import jax
import jax.numpy as jnp
import numpy as np
from jax import lax
from jax.experimental import pallas as pl
from jax.experimental.pallas import tpu as pltpu
from jax.sharding import PartitionSpec as P

bf16 = jnp.bfloat16
f32 = jnp.float32
MESH = pl.DeviceIdType.MESH

HEADS = 8
HEAD = 16
D = 128
FF = 256
WIN = 12
SLOTS = WIN * WIN
LANES = HEADS * SLOTS
STEP = 10
beta_one = 0.9
beta_two = 0.999
learn_rate = 0.2
weight_decay = 0.01
epsilon = 1e-06
clip_bound = 1.0

L1 = dict(q=0, k=128, v=256, o=384, e=512, r=768, p=1024, n=1168)
L0_FF = dict(e=0, r=256)
L0_REST = dict(q=0, k=128, v=256, o=384, p=512, n=656)
SET_ROWS = (1176, 512, 664)

TILES = tuple((a, a + 128) for a in range(0, LANES, 128))


def nt(a, b):
    return lax.dot_general(a, b, (((1,), (1,)), ((), ())), preferred_element_type=f32)


def tn(a, b):
    return lax.dot_general(a, b, (((0,), (0,)), ((), ())), preferred_element_type=f32)


def nn(a, b):
    return jnp.dot(a, b, preferred_element_type=f32)


def head_blocks(block):
    lane = lax.broadcasted_iota(jnp.int32, block.shape, 1)
    parts = []
    for h in range(HEADS):
        keep = (lane >= h * HEAD) & (lane < (h + 1) * HEAD)
        parts.append(jnp.where(keep, block, jnp.zeros_like(block)))
    return jnp.concatenate(parts, axis=0)


def merged(full):
    lane = lax.broadcasted_iota(jnp.int32, (SLOTS, D), 1)
    block = full[0:SLOTS]
    for h in range(1, HEADS):
        block = jnp.where(lane >= h * HEAD, full[h * SLOTS : (h + 1) * SLOTS], block)
    return block


def diagonal(full):
    return jnp.concatenate(
        [full[h * HEAD : (h + 1) * HEAD, h * SLOTS : (h + 1) * SLOTS] for h in range(HEADS)], axis=0
    )


def chunk_rows(rows, parts):
    return (-(-rows // parts) + 7) // 8 * 8


def main_kernel(
    strips,
    windows,
    n_grid,
    feat_in,
    codes_in,
    cot_in,
    attend_in,
    output_in,
    expand_in,
    reduce_in,
    position_in,
    norms_in,
    block_out,
    input_grad,
    grads_one,
    grads_ff,
    grads_rest,
    feat,
    codes_v,
    cot,
    attend_w,
    output_w,
    expand_w,
    reduce_w,
    position,
    norms,
    wa,
    wo,
    we,
    wr,
    xt,
    mi,
    qs,
    ks,
    vs,
    probs,
    att,
    first_b,
    xh1,
    rs1,
    act,
    dgelu,
    xh2,
    rs2,
    crow,
    ccol,
    ctab,
    field,
    wide,
    shifted,
    scores_s,
    d_br2,
    d_hid,
    d_br,
    d_att,
    d_res,
    ds_s,
    d_q,
    d_k,
    d_v,
    csend,
    crecv,
    hsend,
    hrecv,
    osend,
    orecv,
    grecv,
    bsend,
    brecv,
    block_v,
    input_v,
    *sums_and_sems,
):
    send_sem, recv_sem, in_sem, out_sem = sums_and_sems[-4:]
    T = windows * SLOTS
    cols = windows * WIN
    stride = cols + 8
    hw = WIN // 2
    hs = hw * WIN
    gi = lax.axis_index("grid")
    si = lax.axis_index("strip")
    core = lax.rem(si, 2)
    zi = lax.div(si, 2)
    n_z = strips // 2
    chips = n_grid * n_z
    chip = gi * n_z + zi
    prev = lax.rem(si + strips - 1, strips)
    nxt = lax.rem(si + 1, strips)
    sib = si + 1 - 2 * core
    others = []
    for dz in range(n_z):
        for dg in range(n_grid):
            if (dz, dg) != (0, 0):
                g_p, z_p = lax.rem(gi + dg, n_grid), lax.rem(zi + dz, n_z)
                others.append((g_p * n_z + z_p, (g_p, z_p * 2 + core)))

    loads = {}
    for i, (src, dst) in enumerate(
        (
            (feat_in, feat),
            (codes_in, codes_v),
            (attend_in, attend_w),
            (position_in, position),
            (output_in, output_w),
            (expand_in, expand_w),
            (reduce_in, reduce_w),
            (norms_in, norms),
            (cot_in, cot),
        )
    ):
        loads[i] = pltpu.make_async_copy(src, dst, in_sem.at[i])
        loads[i].start()

    barrier = pltpu.get_barrier_semaphore()
    peers = [(gi, prev), (gi, nxt), (gi, sib)] + [device for _, device in others]
    for peer in peers:
        pl.semaphore_signal(barrier, inc=1, device_id=peer, device_id_type=MESH)
    pl.semaphore_wait(barrier, len(peers))

    def remote(src, dst, index, device):
        return pltpu.make_async_remote_copy(
            src_ref=src,
            dst_ref=dst,
            send_sem=send_sem.at[index],
            recv_sem=recv_sem.at[index],
            device_id=device,
            device_id_type=MESH,
        )

    class Total:
        def __init__(self, number):
            self.g, self.s1, self.r1, self.s2, self.r2, self.out = sums_and_sems[
                number * 6 : number * 6 + 6
            ]
            self.c = chunk_rows(SET_ROWS[number], 2 * chips)
            self.sem = 5 + number * 2 * chips

        def rows(self, half, j):
            return pl.ds(pl.multiple_of((half * chips + j) * self.c, 8), self.c)

        def to_sibling(self):
            used = SET_ROWS[number_of(self)]
            if used < 2 * chips * self.c:
                self.g[used:] = jnp.zeros((2 * chips * self.c - used, D), f32)
            for j in range(chips):
                self.s1[j] = self.g[self.rows(1 - core, j)].astype(bf16)
            self.first = remote(self.s1, self.r1, self.sem, (gi, sib))
            self.first.start()

        def to_chips(self):
            self.first.wait()
            for j in range(chips):
                both = self.g[self.rows(core, j)] + self.r1[j].astype(f32)
                self.s2[j] = both.astype(bf16)
            self.copies = []
            for i, (number, device) in enumerate(others):
                copy = remote(self.s2.at[number], self.r2.at[chip], self.sem + 1 + i, device)
                copy.start()
                self.copies.append(copy)
            self.r2[chip] = self.s2[chip]

        def spread(self):
            for copy in self.copies:
                copy.wait()
            total = self.r2[0].astype(f32)
            for j in range(1, chips):
                total = total + self.r2[j].astype(f32)
            self.out[core, chip] = total.astype(bf16)
            self.copies = []
            for i, (number, device) in enumerate(others):
                mine = self.out.at[core, chip]
                copy = remote(mine, mine, self.sem + chips + i, device)
                copy.start()
                self.copies.append(copy)

        def share(self):
            for copy in self.copies:
                copy.wait()
            mine = self.out.at[core]
            self.last = remote(mine, mine, self.sem + 2 * chips - 1, (gi, sib))
            self.last.start()

        def done(self):
            self.last.wait()

    totals = [Total(n) for n in range(3)]
    number_of = totals.index
    homes = (
        {"e": (totals[1], L0_FF), "r": (totals[1], L0_FF)},
        {},
    )

    def put(l, name, value, rows):
        total, table = homes[l].get(name, (totals[2], L0_REST) if l == 0 else (totals[0], L1))
        total.g[table[name] : table[name] + rows] = value

    cot_copy = remote(cot_in.at[pl.ds(0, hw)], grecv, 1, (gi, prev))
    cot_copy.start()
    loads[1].wait()
    csend[...] = jnp.zeros((16, 128), f32)
    for r in range(WIN):
        csend[r : r + 1, 0:cols] = codes_v[r].astype(f32)
    codes_copy = remote(csend, crecv, 0, (gi, prev))
    codes_copy.start()

    def code_tables(l, table):
        low = table.astype(bf16)
        lane = lax.broadcasted_iota(jnp.int32, (16, LANES), 1).astype(f32)
        row = lax.broadcasted_iota(jnp.int32, (16, LANES), 0).astype(f32)
        slot = lane - SLOTS * jnp.floor((lane + 0.5) * (1.0 / SLOTS))
        slot_r = jnp.floor((slot + 0.5) * (1.0 / WIN))
        slot_c = slot - WIN * slot_r
        pick_r = (slot_r == row).astype(bf16)
        ctab[...] = tn(low, pick_r)
        pick_c = (slot_c == row).astype(f32)[0:WIN]
        for w in range(windows):
            part = ctab[w * WIN : (w + 1) * WIN, :]
            crow[l, w] = jnp.sum(part * pick_c, axis=0, keepdims=True)
        token = lax.broadcasted_iota(jnp.int32, (SLOTS, 128), 0).astype(f32)
        place = lax.broadcasted_iota(jnp.int32, (SLOTS, 128), 1).astype(f32)
        token_r = jnp.floor((token + 0.5) * (1.0 / WIN))
        token_c = token - WIN * token_r
        row_of = (token_r == place).astype(bf16)[:, 0:16]
        spread = nn(row_of, low)
        for w in range(windows):
            chosen = jnp.where(place == token_c + w * WIN, spread, 0.0)
            value = jnp.sum(chosen, axis=1, keepdims=True)
            ccol[l, w * SLOTS : (w + 1) * SLOTS] = jnp.broadcast_to(value, (SLOTS, 128))

    def window_rows(w):
        return slice(w * SLOTS, (w + 1) * SLOTS)

    def layer_forward(l):
        x = xt[l]
        m = (x.astype(f32) + jnp.concatenate([position[l]] * windows, axis=0)).astype(bf16)
        mi[l] = m
        qk = nn(m, wa[l, :, 0 : 2 * D])
        qs[l] = (qk[:, 0:D] * HEAD ** (-0.5)).astype(bf16)
        ks[l] = qk[:, D : 2 * D].astype(bf16)
        vs[l] = nn(x, wa[l, :, 2 * D : 3 * D]).astype(bf16)

        for w in range(windows):
            rows = window_rows(w)
            qb = head_blocks(qs[l, rows])
            scores_s[...] = nt(ks[l, rows], qb)
            cc = ccol[l, rows]
            cr = crow[l, w]
            for a, b in TILES:
                scores = jnp.where(cc == cr[:, a:b], scores_s[:, a:b], -1000000000.0)
                top = jnp.max(scores, axis=0, keepdims=True)
                weights = jnp.exp(scores - top)
                total = jnp.sum(weights, axis=0, keepdims=True)
                probs[l, rows, a:b] = (weights * (1.0 / total)).astype(bf16)
            att[l, rows] = merged(tn(probs[l, rows], vs[l, rows])).astype(bf16)

        r = xt[l].astype(f32) + nn(att[l], wo[l])
        c = r - jnp.mean(r, axis=1, keepdims=True)
        s = lax.rsqrt(jnp.mean(c * c, axis=1, keepdims=True) + 1e-05)
        n = c * s
        xh1[l] = n
        rs1[l] = jnp.broadcast_to(s, n.shape)
        first = n * norms[l, 0:1] + norms[l, 1:2]
        fb = first.astype(bf16)
        first_b[l] = fb
        h = nn(fb, we[l])
        h2 = h * h
        t = jnp.tanh(0.7978845608028654 * h * (1.0 + 0.044715 * h2))
        act_b = (0.5 * h * (1.0 + t)).astype(bf16)
        act[l] = act_b
        dgelu[l] = 0.5 * (1.0 + t) + 0.5 * h * (1.0 - t * t) * (
            0.7978845608028654 * (1.0 + 3.0 * 0.044715 * h2)
        )
        r = first + nn(act_b, wr[l])
        c = r - jnp.mean(r, axis=1, keepdims=True)
        s = lax.rsqrt(jnp.mean(c * c, axis=1, keepdims=True) + 1e-05)
        n = c * s
        xh2[l] = n
        rs2[l] = jnp.broadcast_to(s, n.shape)
        second = n * norms[l, 2:3] + norms[l, 3:4]
        second = jnp.where(ccol[l] > 0.0, second, 0.0)
        wide[...] = second.astype(bf16).astype(f32)

    def norm_back(d, gain, n, s):
        dn = d * gain
        m1 = jnp.mean(dn, axis=1, keepdims=True)
        m2 = jnp.mean(dn * n, axis=1, keepdims=True)
        return s * (dn - m1 - n * m2)

    def dense_backward(l):
        d = jnp.where(ccol[l] > 0.0, wide[...], 0.0)
        n2 = xh2[l]
        bias2 = jnp.sum(d, axis=0, keepdims=True)
        gain2 = jnp.sum(d * n2, axis=0, keepdims=True)
        d2 = norm_back(d, norms[l, 2:3], n2, rs2[l])
        b2 = d2.astype(bf16)
        d_br2[...] = b2
        dh = (nt(b2, wr[l]) * dgelu[l]).astype(bf16)
        d_hid[...] = dh
        d1 = d2 + nt(dh, we[l])
        n1 = xh1[l]
        bias1 = jnp.sum(d1, axis=0, keepdims=True)
        gain1 = jnp.sum(d1 * n1, axis=0, keepdims=True)
        dr = norm_back(d1, norms[l, 0:1], n1, rs1[l])
        d_res[...] = dr
        b1 = dr.astype(bf16)
        d_br[...] = b1
        d_att[...] = nt(b1, wo[l]).astype(bf16)
        lines = [gain1, bias1, gain2, bias2, jnp.zeros((4, D), f32)]
        put(l, "n", jnp.concatenate(lines, axis=0), 8)

    def feed_forward_grads(l):
        put(l, "r", tn(act[l], d_br2[...]), FF)
        d_expand = tn(first_b[l], d_hid[...])
        put(l, "e", jnp.concatenate([d_expand[:, 0:D], d_expand[:, D : 2 * D]], axis=0), FF)

    def attention_backward(l):
        for w in range(windows):
            rows = window_rows(w)
            db = head_blocks(d_att[rows])
            qb = head_blocks(qs[l, rows])
            d_probs = nt(vs[l, rows], db)
            for a, b in TILES:
                dp = d_probs[:, a:b]
                p = probs[l, rows, a:b].astype(f32)
                ds = p * (dp - jnp.sum(dp * p, axis=0, keepdims=True))
                ds_s[rows, a:b] = ds.astype(bf16)
            d_v[rows] = nn(probs[l, rows], db).astype(bf16)
            ds = ds_s[rows]
            d_k[rows] = nn(ds, qb).astype(bf16)
            full = nn(ks[l, rows].T, ds)
            d_q[rows] = (diagonal(full).T * HEAD ** (-0.5)).astype(bf16)

    def attention_grads(l):
        put(l, "o", tn(att[l], d_br[...]), D)
        put(l, "q", tn(mi[l], d_q[...]), D)
        put(l, "k", tn(mi[l], d_k[...]), D)
        put(l, "v", tn(xt[l], d_v[...]), D)
        d_pos = jnp.zeros((SLOTS, D), f32)
        for part, columns in ((d_q, slice(0, D)), (d_k, slice(D, 2 * D))):
            total = part[0:SLOTS].astype(f32)
            for w in range(1, windows):
                total = total + part[window_rows(w)].astype(f32)
            high = total.astype(bf16)
            low = (total - high.astype(f32)).astype(bf16)
            d_pos = d_pos + nt(high, wa[l, :, columns]) + nt(low, wa[l, :, columns])
        put(l, "p", d_pos, SLOTS)

    def input_gradient(l):
        d = d_res[...] + nt(d_q[...], wa[l, :, 0:D]) + nt(d_k[...], wa[l, :, D : 2 * D])
        wide[...] = d + nt(d_v[...], wa[l, :, 2 * D : 3 * D])

    loads[0].wait()
    for r in range(WIN):
        field[r * stride : r * stride + cols] = feat[r].astype(f32)
    for w in range(windows):
        for r in range(WIN):
            a = w * SLOTS + r * WIN
            wide[a : a + WIN] = field[r * stride + w * WIN : r * stride + (w + 1) * WIN]
    xt[0] = wide[...].astype(bf16)
    code_tables(0, csend[...])
    for i in range(2, 8):
        loads[i].wait()

    def lower(l):
        wa[l] = attend_w[l].astype(bf16)
        wo[l] = output_w[l].astype(bf16)
        we[l] = expand_w[l].astype(bf16)
        wr[l] = reduce_w[l].astype(bf16)

    lower(0)
    layer_forward(0)

    for w in range(windows):
        hsend[w * hs : (w + 1) * hs] = wide[w * SLOTS : w * SLOTS + hs].astype(bf16)
    halo_copy = remote(hsend, hrecv, 2, (gi, prev))
    halo_copy.start()

    def wrap(rows):
        for r in rows:
            field[r * stride + cols : r * stride + cols + hw] = field[r * stride : r * stride + hw]

    def to_shifted(target, rows):
        wrap(rows)
        for w in range(windows):
            for r in rows:
                a = w * SLOTS + r * WIN
                b = r * stride + w * WIN + hw
                target[a : a + WIN] = field[b : b + WIN]

    loads[8].wait()
    cot_copy.wait()
    for r in range(hw):
        field[r * stride : r * stride + cols] = cot[r + hw].astype(f32)
        field[(r + hw) * stride : (r + hw) * stride + cols] = grecv[r].astype(f32)
    to_shifted(shifted, range(WIN))
    lower(1)
    codes_copy.wait()
    own = csend[...]
    other = crecv[...]
    table = jnp.concatenate([own[hw:WIN], other[0:hw], jnp.zeros((4, 128), f32)], axis=0)
    table = jnp.concatenate(
        [table[:, hw:cols], table[:, 0:hw], jnp.zeros((16, 128 - cols), f32)], axis=1
    )
    code_tables(1, table)
    for w in range(windows):
        for r in range(hw):
            a = w * SLOTS + (r + hw) * WIN
            field[r * stride + w * WIN : r * stride + (w + 1) * WIN] = wide[a : a + WIN]
    to_shifted(wide, range(hw))
    halo_copy.wait()
    d_res[0 : windows * hs] = hrecv[...].astype(f32)
    for w in range(windows):
        for r in range(hw):
            a = w * hs + r * WIN
            b = (r + hw) * stride
            field[b + w * WIN : b + (w + 1) * WIN] = d_res[a : a + WIN]
    to_shifted(wide, range(hw, WIN))
    xt[1] = wide[...].astype(bf16)
    layer_forward(1)

    for w in range(windows):
        osend[w * hs : (w + 1) * hs] = wide[w * SLOTS + hs : (w + 1) * SLOTS].astype(bf16)
    out_copy = remote(osend, orecv, 3, (gi, nxt))
    out_copy.start()

    def from_shifted(source, source_rows, first_row):
        for w in range(windows):
            for r in range(hw):
                a = w * source_rows + r * WIN
                b = (r + first_row) * stride + w * WIN + hw
                field[b : b + WIN] = source[a : a + WIN]
        for r in range(first_row, first_row + hw):
            field[r * stride : r * stride + hw] = field[r * stride + cols : r * stride + cols + hw]

    from_shifted(wide, SLOTS, hw)
    for r in range(hw, WIN):
        block_v[r] = field[r * stride : r * stride + cols].astype(bf16)

    wide[...] = shifted[...]
    dense_backward(1)
    attention_backward(1)
    input_gradient(1)

    for w in range(windows):
        bsend[w * hs : (w + 1) * hs] = wide[w * SLOTS + hs : (w + 1) * SLOTS].astype(bf16)
    back_copy = remote(bsend, brecv, 4, (gi, nxt))
    back_copy.start()
    from_shifted(wide, SLOTS, hw)
    feed_forward_grads(1)
    attention_grads(1)
    totals[0].to_sibling()
    back_copy.wait()
    wide[0 : windows * hs] = brecv[...].astype(f32)
    from_shifted(wide, hs, 0)
    for w in range(windows):
        for r in range(WIN):
            a = w * SLOTS + r * WIN
            wide[a : a + WIN] = field[r * stride + w * WIN : r * stride + (w + 1) * WIN]
    wide[...] = wide[...].astype(bf16).astype(f32)

    totals[0].to_chips()
    dense_backward(0)
    feed_forward_grads(0)
    totals[1].to_sibling()
    totals[0].spread()
    totals[1].to_chips()
    attention_backward(0)
    totals[0].share()
    totals[1].spread()
    attention_grads(0)
    totals[2].to_sibling()
    input_gradient(0)
    totals[2].to_chips()
    totals[1].share()
    for w in range(windows):
        for r in range(WIN):
            a = w * SLOTS + r * WIN
            field[r * stride + w * WIN : r * stride + (w + 1) * WIN] = wide[a : a + WIN]
    for r in range(WIN):
        input_v[r] = field[r * stride : r * stride + cols]
    out_copy.wait()
    wide[0 : windows * hs] = orecv[...].astype(f32)
    from_shifted(wide, hs, 0)
    for r in range(hw):
        block_v[r] = field[r * stride : r * stride + cols].astype(bf16)
    stores = [
        pltpu.make_async_copy(block_v, block_out, out_sem.at[0]),
        pltpu.make_async_copy(input_v, input_grad, out_sem.at[1]),
    ]
    for store in stores:
        store.start()
    totals[0].done()
    totals[1].done()
    stores.append(pltpu.make_async_copy(totals[0].out, grads_one, out_sem.at[2]))
    stores.append(pltpu.make_async_copy(totals[1].out, grads_ff, out_sem.at[3]))
    for store in stores[2:]:
        store.start()
    totals[2].spread()
    totals[2].share()
    totals[2].done()
    stores.append(pltpu.make_async_copy(totals[2].out, grads_rest, out_sem.at[4]))
    stores[4].start()
    for store in stores:
        store.wait()


def main_call(strips, windows, cols, n_grid):
    T = windows * SLOTS
    hw = WIN // 2
    chips = n_grid * strips // 2
    vm = pltpu.VMEM
    hs = windows * hw * WIN
    scratch = [
        vm((WIN, cols, D), bf16),
        vm((WIN, 1, cols), jnp.int32),
        vm((WIN, cols, D), bf16),
        vm((2, D, 3 * D), f32),
        vm((2, D, D), f32),
        vm((2, D, FF), f32),
        vm((2, FF, D), f32),
        vm((2, SLOTS, D), f32),
        vm((2, 4, D), f32),
        vm((2, D, 3 * D), bf16),
        vm((2, D, D), bf16),
        vm((2, D, FF), bf16),
        vm((2, FF, D), bf16),
        vm((2, T, D), bf16),
        vm((2, T, D), bf16),
        vm((2, T, D), bf16),
        vm((2, T, D), bf16),
        vm((2, T, D), bf16),
        vm((2, T, LANES), bf16),
        vm((2, T, D), bf16),
        vm((2, T, D), bf16),
        vm((2, T, D), f32),
        vm((2, T, D), f32),
        vm((2, T, FF), bf16),
        vm((2, T, FF), f32),
        vm((2, T, D), f32),
        vm((2, T, D), f32),
        vm((2, windows, 1, LANES), f32),
        vm((2, T, D), f32),
        vm((128, LANES), f32),
        vm((WIN * (cols + 8), D), f32),
        vm((T, D), f32),
        vm((T, D), f32),
        vm((SLOTS, LANES), f32),
        vm((T, D), bf16),
        vm((T, FF), bf16),
        vm((T, D), bf16),
        vm((T, D), bf16),
        vm((T, D), f32),
        vm((T, LANES), bf16),
        vm((T, D), bf16),
        vm((T, D), bf16),
        vm((T, D), bf16),
        vm((16, 128), f32),
        vm((16, 128), f32),
        vm((hs, D), bf16),
        vm((hs, D), bf16),
        vm((hs, D), bf16),
        vm((hs, D), bf16),
        vm((hw, cols, D), bf16),
        vm((hs, D), bf16),
        vm((hs, D), bf16),
        vm((WIN, cols, D), bf16),
        vm((WIN, cols, D), f32),
    ]
    outs = []
    for rows in SET_ROWS:
        c = chunk_rows(rows, 2 * chips)
        scratch += [
            vm((2 * chips * c, D), f32),
            vm((chips, c, D), bf16),
            vm((chips, c, D), bf16),
            vm((chips, c, D), bf16),
            vm((chips, c, D), bf16),
            vm((2, chips, c, D), bf16),
        ]
        outs.append(jax.ShapeDtypeStruct((2, chips, c, D), bf16))
    copies = 5 + 3 * 2 * chips
    scratch += [pltpu.SemaphoreType.DMA((n,)) for n in (copies, copies, 9, 5)]
    far = pl.BlockSpec(memory_space=pl.ANY)
    return pl.pallas_call(
        functools.partial(main_kernel, strips, windows, n_grid),
        out_shape=(
            jax.ShapeDtypeStruct((WIN, cols, D), bf16),
            jax.ShapeDtypeStruct((WIN, cols, D), f32),
            *outs,
        ),
        in_specs=[far] * 9,
        out_specs=(far,) * 5,
        scratch_shapes=scratch,
        compiler_params=pltpu.CompilerParams(
            collective_id=0, has_side_effects=True, vmem_limit_bytes=60 * 1024 * 1024
        ),
    )


def lamb_kernel(*refs):
    grads_far = refs[0:3]
    block_in, input_in = refs[3:5]
    states_far = refs[5:23]
    block_out, input_out = refs[23:25]
    results_far = refs[25:43]
    clip_out, norms_out = refs[43:45]
    grads_near = refs[45:48]
    states = refs[48:66]
    results = refs[66:84]
    block_near, input_near = refs[84:86]
    grad_sem, state_sem, out_sem, cell_sem = refs[86:90]
    cell_loads = [
        pltpu.make_async_copy(block_in, block_near, cell_sem.at[0]),
        pltpu.make_async_copy(input_in, input_near, cell_sem.at[1]),
    ]
    cell_stores = [
        pltpu.make_async_copy(block_near, block_out, cell_sem.at[2]),
        pltpu.make_async_copy(input_near, input_out, cell_sem.at[3]),
    ]
    grad_loads = [
        pltpu.make_async_copy(grads_far[i], grads_near[i], grad_sem.at[i]) for i in range(3)
    ]
    loads = [
        pltpu.make_async_copy(states_far[i], states[i], state_sem.at[i]) for i in range(18)
    ]
    stores = [
        pltpu.make_async_copy(results[i], results_far[i], out_sem.at[i]) for i in range(18)
    ]
    for copy in grad_loads:
        copy.start()
    for index in range(6):
        for kind in range(3):
            loads[6 * kind + index].start()
    for copy in cell_loads:
        copy.start()
    for copy in grad_loads:
        copy.wait()
    grads = [g[...].astype(f32).reshape(-1, D) for g in grads_near]
    clip_norm = jnp.sqrt(sum(jnp.sum(g * g, keepdims=True) for g in grads))
    clip_out[...] = clip_norm
    factor = clip_bound / jnp.maximum(clip_norm, clip_bound)
    fix_one = 1.0 / (1.0 - beta_one**STEP)
    fix_two = 1.0 / (1.0 - beta_two**STEP)

    def grad_rows(l, name, start, rows):
        if l == 1:
            number, table = 0, L1
        elif name in L0_FF:
            number, table = 1, L0_FF
        else:
            number, table = 2, L0_REST
        return grads[number][table[name] + start : table[name] + start + rows]

    def step(index, where, grad, decay):
        grad = grad * factor
        old = states[index][where]
        moment = beta_one * states[6 + index][where] + (1.0 - beta_one) * grad
        square = beta_two * states[12 + index][where] + (1.0 - beta_two) * grad * grad
        results[6 + index][where] = moment
        results[12 + index][where] = square
        direction = moment * fix_one / (jnp.sqrt(square * fix_two) + epsilon)
        if decay:
            direction = direction + weight_decay * old
        return old, direction

    found = {}
    for index, names, height in (
        (0, "qkv", D),
        (1, "o", D),
        (2, "ee", D),
        (3, "r", FF),
        (4, "p", SLOTS),
    ):
        for kind in range(3):
            loads[6 * kind + index].wait()
        for l in range(2):
            parts = []
            for b, name in enumerate(names):
                where = (l, slice(None), slice(b * D, (b + 1) * D))
                grad = grad_rows(l, name, b * D if name == "e" else 0, height)
                parts.append((where,) + step(index, where, grad, True))
            weight_norm = jnp.sqrt(sum(jnp.sum(old * old, keepdims=True) for _, old, _ in parts))
            step_norm = jnp.sqrt(sum(jnp.sum(d * d, keepdims=True) for _, _, d in parts))
            scale = learn_rate * weight_norm / (step_norm + epsilon)
            for where, old, direction in parts:
                results[index][where] = old - scale * direction
            found[l, index] = (weight_norm, step_norm)
        for kind in range(3):
            stores[6 * kind + index].start()
        if index < 2:
            cell_loads[index].wait()
            cell_stores[index].start()
    for kind in range(3):
        loads[6 * kind + 5].wait()
    for l in range(2):
        old, direction = step(5, (l,), grad_rows(l, "n", 0, 4), False)
        weight_norm = jnp.sqrt(jnp.sum(old * old, axis=1, keepdims=True))
        step_norm = jnp.sqrt(jnp.sum(direction * direction, axis=1, keepdims=True))
        results[5][l] = old - learn_rate * weight_norm / (step_norm + epsilon) * direction
        for r in range(4):
            found[l, 5 + r] = (weight_norm[r : r + 1], step_norm[r : r + 1])
        row = lax.broadcasted_iota(jnp.int32, (2, 9), 0)
        lane = lax.broadcasted_iota(jnp.int32, (2, 9), 1)
        table = jnp.zeros((2, 9), f32)
        for t in range(9):
            for j in range(2):
                value = jnp.broadcast_to(found[l, t][j], (2, 9))
                table = jnp.where((row == j) & (lane == t), value, table)
        norms_out[l] = table
    for kind in range(3):
        stores[6 * kind + 5].start()
    for copy in stores + cell_stores:
        copy.wait()


def lamb_call(grads, block_output, input_grad, weights, firsts, seconds):
    whole = pl.BlockSpec(memory_space=pltpu.VMEM)
    far = pl.BlockSpec(memory_space=pl.ANY)
    like = lambda a: jax.ShapeDtypeStruct(a.shape, a.dtype)
    states = [*weights, *firsts, *seconds]
    out = [like(block_output), like(input_grad)]
    out += [like(a) for a in states]
    out += [jax.ShapeDtypeStruct((1, 1), f32), jax.ShapeDtypeStruct((2, 2, 9), f32)]
    near = [
        pltpu.VMEM(a.shape, a.dtype)
        for a in (*grads, *states, *states, block_output, input_grad)
    ]
    return pl.pallas_call(
        lamb_kernel,
        out_shape=out,
        in_specs=[far] * 23,
        out_specs=[far] * 20 + [whole] * 2,
        scratch_shapes=near + [pltpu.SemaphoreType.DMA((n,)) for n in (3, 18, 18, 4)],
        compiler_params=pltpu.CompilerParams(vmem_limit_bytes=60 * 1024 * 1024),
    )(*grads, block_output, input_grad, *states)


def body(mesh, features, cell_frame, cotangent, *rest):
    weights, firsts, seconds = rest[0:6], rest[6:12], rest[12:18]
    cols = features.shape[2]
    call = main_call(mesh.shape["strip"], cols // WIN, cols, mesh.shape["grid"])
    cell_frame = cell_frame.reshape(WIN, 1, cols)
    block_output, input_grad, *grads = call(features[0], cell_frame, cotangent[0], *weights)
    out = lamb_call(grads, block_output, input_grad, weights, firsts, seconds)
    norms = jnp.swapaxes(out[21], 1, 2)
    return (out[0][None], out[1][None], *out[2:20], out[20].reshape(()), norms)


def solution(mesh):
    cells = P("grid", "strip", None, None)
    return jax.shard_map(
        functools.partial(body, mesh),
        mesh=mesh,
        in_specs=(cells, P("grid", "strip", None), cells) + (P(),) * 18,
        out_specs=(cells, cells) + (P(),) * 20,
        check_vma=False,
    )
```

time: 101 us -> 64.2 us (0.64)
  Pallas kernels: 86.3 us -> 63.2 us
  local copies, waits for them, and re-layouts: 13.8 us -> 0 us
    pallas_call x2, Pallas kernels: 86.3 us -> 63.2 us  [the longest x1 56.7 us: body(): call(features[0], cell_frame, cotangent[0], *weights)]
    unnamed x44 -> x0, local copies, waits for them, and re-layouts: 13.8 us -> none
where the time goes in v1:
time: 64.2 us; the launch traced here: 64.1 us
  Pallas kernels  63.2 us (98%)
  between operations  0.83 us (1%)
    pallas_call x1, Pallas kernels, body(): call(features[0], cell_frame, cotangent[0], *weights)  56.7 us
    pallas_call x1, Pallas kernels, lamb_call(): pl.pallas_call(lamb_kernel, out_shape=out, in_specs=[far] * 23, out_specs...  6.55 us

profile of v1, /device:TPU:0, one launch (start us, length us, event | category | flops | bytes accessed | tf_op | source)
XLA Modules:
  0.0 64.1 jit_solution(3406951253995381077)
XLA Ops:
  0.7 56.7 %shard_map.372 = (bf16[12,72,128]{2,1,0:T(8,128)(2,1)}, f32[12,72,128]{2,1,0:T(8,128)}, bf16[2,16,40,128]{3,2,1,0:T(8,128)(2,1)}, bf16[2,16,16,128]{3,2,1,0:T(8,128)(2,1)}, bf16[2,16,24,128]{3,2,1,0:T(8,128)(2,1)}) custom-call(bf16[12,72,128]{2,1,0:T(8,128)(2,1)} %bitcast.7, s32[12,1,72]{2,1,0:T(1,128)} %bitcast.9, bf16[12,72,128]{2,1,0:T(8,128)(2,1)} %bitcast.8, ...), custom_call_target="tpu_custom_call" | custom-call | tf_op jit(solution)/shard_map/pallas_call | solution.py:820
  57.3 6.5 %shard_map.373 = (bf16[12,72,128]{2,1,0:T(8,128)(2,1)}, f32[12,72,128]{2,1,0:T(8,128)}, f32[2,128,384]{2,1,0:T(8,128)}, f32[2,128,128]{2,1,0:T(8,128)}, f32[2,12...) custom-call(bf16[2,16,40,128]{3,2,1,0:T(8,128)(2,1)} %get-tuple-elem, ...), custom_call_target="tpu_custom_call" | custom-call | tf_op jit(solution)/shard_map/pallas_call | solution.py:805

commit v2 on v1

v2 whole, which is shorter than its diff:
```python
import functools

import jax
import jax.numpy as jnp
import numpy as np
from jax import lax
from jax.experimental import pallas as pl
from jax.experimental.pallas import tpu as pltpu
from jax.sharding import PartitionSpec as P

bf16 = jnp.bfloat16
f32 = jnp.float32
MESH = pl.DeviceIdType.MESH

HEADS = 8
HEAD = 16
D = 128
FF = 256
WIN = 12
SLOTS = WIN * WIN
LANES = HEADS * SLOTS
STEP = 10
beta_one = 0.9
beta_two = 0.999
learn_rate = 0.2
weight_decay = 0.01
epsilon = 1e-06
clip_bound = 1.0

L1 = dict(q=0, k=128, v=256, o=384, e=512, r=768, p=1024, n=1168)
L0_FF = dict(e=0, r=256)
L0_REST = dict(q=0, k=128, v=256, o=384, p=512, n=656)
SET_ROWS = (1176, 512, 664)

FORWARD_ZERO = ((0, 2), (2, 4), (4, 6))
FORWARD_ONE = ((0, 3), (3, 6))
BACKWARD_ONE = ((0, 2), (2, 4), (4, 6))
BACKWARD_ZERO = (((1, 4),), ((4, 6), (0, 1)))
COPIES = 9

TILES = tuple((a, a + 128) for a in range(0, LANES, 128))


def nt(a, b):
    return lax.dot_general(a, b, (((1,), (1,)), ((), ())), preferred_element_type=f32)


def tn(a, b):
    return lax.dot_general(a, b, (((0,), (0,)), ((), ())), preferred_element_type=f32)


def nn(a, b):
    return jnp.dot(a, b, preferred_element_type=f32)


def head_blocks(block):
    lane = lax.broadcasted_iota(jnp.int32, block.shape, 1)
    parts = []
    for h in range(HEADS):
        keep = (lane >= h * HEAD) & (lane < (h + 1) * HEAD)
        parts.append(jnp.where(keep, block, jnp.zeros_like(block)))
    return jnp.concatenate(parts, axis=0)


def merged(full):
    lane = lax.broadcasted_iota(jnp.int32, (SLOTS, D), 1)
    block = full[0:SLOTS]
    for h in range(1, HEADS):
        block = jnp.where(lane >= h * HEAD, full[h * SLOTS : (h + 1) * SLOTS], block)
    return block


def diagonal(full):
    return jnp.concatenate(
        [full[h * HEAD : (h + 1) * HEAD, h * SLOTS : (h + 1) * SLOTS] for h in range(HEADS)], axis=0
    )


def chunk_rows(rows, parts):
    return (-(-rows // parts) + 7) // 8 * 8


def main_kernel(
    strips,
    windows,
    n_grid,
    feat_in,
    codes_in,
    cot_in,
    attend_in,
    output_in,
    expand_in,
    reduce_in,
    position_in,
    norms_in,
    *refs,
):
    states_in, refs = refs[:12], refs[12:]
    outs, refs = refs[:23], refs[23:]
    run(strips, windows, n_grid, feat_in, codes_in, cot_in, attend_in, output_in, expand_in,
        reduce_in, position_in, norms_in, states_in, outs, *refs)


def run(
    strips,
    windows,
    n_grid,
    feat_in,
    codes_in,
    cot_in,
    attend_in,
    output_in,
    expand_in,
    reduce_in,
    position_in,
    norms_in,
    states_in,
    outs,
    feat,
    codes_v,
    cot,
    wa,
    wo,
    we,
    wr,
    xt,
    mi,
    qs,
    ks,
    vs,
    probs,
    att,
    first_b,
    xh1,
    rs1,
    act,
    dgelu,
    xh2,
    rs2,
    crow,
    ccol,
    ctab,
    field_a,
    field_b,
    field_c,
    field_d,
    wide_a,
    wide_b,
    wide_c,
    wide_d,
    wide_e,
    wide_f,
    wide_g,
    wide_h,
    scores_s,
    d_br2,
    d_hid,
    d_br,
    d_att,
    d_res,
    ds_s,
    d_q,
    d_k,
    d_v,
    csend,
    crecv,
    hsend,
    hrecv,
    osend,
    orecv,
    grecv,
    bsend,
    brecv,
    *sums_and_sems,
):
    send_sem, recv_sem, in_sem, out_sem = sums_and_sems[-4:]
    T = windows * SLOTS
    cols = windows * WIN
    stride = cols + 8
    hw = WIN // 2
    hs = hw * WIN
    gi = lax.axis_index("grid")
    si = lax.axis_index("strip")
    core = lax.rem(si, 2)
    zi = lax.div(si, 2)
    n_z = strips // 2
    chips = n_grid * n_z
    chip = gi * n_z + zi
    prev = lax.rem(si + strips - 1, strips)
    nxt = lax.rem(si + 1, strips)
    sib = si + 1 - 2 * core
    others = []
    for dz in sorted(range(n_z), key=lambda d: -min(d, n_z - d)):
        for dg in reversed(range(n_grid)):
            if (dz, dg) != (0, 0):
                g_p, z_p = lax.rem(gi + dg, n_grid), lax.rem(zi + dz, n_z)
                others.append((g_p * n_z + z_p, (g_p, z_p * 2 + core)))

    block_v, input_v = outs[0:2]
    attend_w, output_w, expand_w, reduce_w, position, norms = outs[5:11]
    loads = {}
    for i, (src, dst) in enumerate(
        (
            (feat_in, feat),
            (codes_in, codes_v),
            (attend_in, attend_w),
            (position_in, position),
            (output_in, output_w),
            (expand_in, expand_w),
            (reduce_in, reduce_w),
            (norms_in, norms),
            (cot_in, cot),
        )
    ):
        loads[i] = pltpu.make_async_copy(src, dst, in_sem.at[i])
        loads[i].start()

    state_loads = []
    for i, (src, dst) in enumerate(zip(states_in, outs[11:23])):
        state_loads.append(pltpu.make_async_copy(src, dst, out_sem.at[i]))

    barrier = pltpu.get_barrier_semaphore()
    peers = [(gi, prev), (gi, nxt), (gi, sib)] + [device for _, device in others]
    for peer in peers:
        pl.semaphore_signal(barrier, inc=1, device_id=peer, device_id_type=MESH)

    def remote(src, dst, index, device):
        return pltpu.make_async_remote_copy(
            src_ref=src,
            dst_ref=dst,
            send_sem=send_sem.at[index],
            recv_sem=recv_sem.at[index],
            device_id=device,
            device_id_type=MESH,
        )

    class Total:
        def __init__(self, number):
            self.g, self.s1, self.r1, self.s2, self.r2 = sums_and_sems[
                number * 5 : number * 5 + 5
            ]
            self.out = outs[2 + number]
            self.c = chunk_rows(SET_ROWS[number], 2 * chips)
            self.sem = COPIES + number * 2 * chips

        def rows(self, half, j):
            return pl.ds(pl.multiple_of((half * chips + j) * self.c, 8), self.c)

        def to_sibling(self):
            used = SET_ROWS[number_of(self)]
            if used < 2 * chips * self.c:
                self.g[used:] = jnp.zeros((2 * chips * self.c - used, D), f32)
            for j in range(chips):
                self.s1[j] = self.g[self.rows(1 - core, j)].astype(bf16)
            self.first = remote(self.s1, self.r1, self.sem, (gi, sib))
            self.first.start()

        def to_chips(self):
            self.first.wait()
            for j in range(chips):
                both = self.g[self.rows(core, j)] + self.r1[j].astype(f32)
                self.s2[j] = both.astype(bf16)
            self.copies = []
            for i, (number, device) in enumerate(others):
                copy = remote(self.s2.at[number], self.r2.at[chip], self.sem + 1 + i, device)
                copy.start()
                self.copies.append(copy)
            self.r2[chip] = self.s2[chip]

        def spread(self):
            for copy in self.copies:
                copy.wait()
            total = self.r2[0].astype(f32)
            for j in range(1, chips):
                total = total + self.r2[j].astype(f32)
            self.out[core, chip] = total.astype(bf16)
            self.copies = []
            for i, (number, device) in enumerate(others):
                mine = self.out.at[core, chip]
                copy = remote(mine, mine, self.sem + chips + i, device)
                copy.start()
                self.copies.append(copy)

        def share(self):
            for copy in self.copies:
                copy.wait()
            mine = self.out.at[core]
            self.last = remote(mine, mine, self.sem + 2 * chips - 1, (gi, sib))
            self.last.start()

        def done(self):
            self.last.wait()

    totals = [Total(n) for n in range(3)]
    number_of = totals.index
    homes = (
        {"e": (totals[1], L0_FF), "r": (totals[1], L0_FF)},
        {},
    )

    def put(l, name, value, rows):
        total, table = homes[l].get(name, (totals[2], L0_REST) if l == 0 else (totals[0], L1))
        total.g[table[name] : table[name] + rows] = value

    def code_tables(l, table):
        low = table.astype(bf16)
        lane = lax.broadcasted_iota(jnp.int32, (16, LANES), 1).astype(f32)
        row = lax.broadcasted_iota(jnp.int32, (16, LANES), 0).astype(f32)
        slot = lane - SLOTS * jnp.floor((lane + 0.5) * (1.0 / SLOTS))
        slot_r = jnp.floor((slot + 0.5) * (1.0 / WIN))
        slot_c = slot - WIN * slot_r
        pick_r = (slot_r == row).astype(bf16)
        ctab[...] = tn(low, pick_r)
        pick_c = (slot_c == row).astype(f32)[0:WIN]
        for w in range(windows):
            part = ctab[w * WIN : (w + 1) * WIN, :]
            crow[l, w] = jnp.sum(part * pick_c, axis=0, keepdims=True)
        token = lax.broadcasted_iota(jnp.int32, (SLOTS, 128), 0).astype(f32)
        place = lax.broadcasted_iota(jnp.int32, (SLOTS, 128), 1).astype(f32)
        token_r = jnp.floor((token + 0.5) * (1.0 / WIN))
        token_c = token - WIN * token_r
        row_of = (token_r == place).astype(bf16)[:, 0:16]
        spread = nn(row_of, low)
        for w in range(windows):
            chosen = jnp.where(place == token_c + w * WIN, spread, 0.0)
            value = jnp.sum(chosen, axis=1, keepdims=True)
            ccol[l, w * SLOTS : (w + 1) * SLOTS] = jnp.broadcast_to(value, (SLOTS, 128))

    def window_rows(w):
        return slice(w * SLOTS, (w + 1) * SLOTS)

    def layer_forward(l, first_window, end, out):
        rows = slice(first_window * SLOTS, end * SLOTS)
        x = xt[l, rows]
        places = jnp.concatenate([position[l]] * (end - first_window), axis=0)
        m = (x.astype(f32) + places).astype(bf16)
        mi[l, rows] = m
        qk = nn(m, wa[l, :, 0 : 2 * D])
        qs[l, rows] = (qk[:, 0:D] * HEAD ** (-0.5)).astype(bf16)
        ks[l, rows] = qk[:, D : 2 * D].astype(bf16)
        vs[l, rows] = nn(x, wa[l, :, 2 * D : 3 * D]).astype(bf16)

        for w in range(first_window, end):
            one = window_rows(w)
            qb = head_blocks(qs[l, one])
            scores_s[w % 2] = nt(ks[l, one], qb)
            cc = ccol[l, one]
            cr = crow[l, w]
            for a, b in TILES:
                scores = jnp.where(cc == cr[:, a:b], scores_s[w % 2, :, a:b], -1000000000.0)
                top = jnp.max(scores, axis=0, keepdims=True)
                weights = jnp.exp(scores - top)
                total = jnp.sum(weights, axis=0, keepdims=True)
                probs[l, one, a:b] = (weights * (1.0 / total)).astype(bf16)
            att[l, one] = merged(tn(probs[l, one], vs[l, one])).astype(bf16)

        r = xt[l, rows].astype(f32) + nn(att[l, rows], wo[l])
        c = r - jnp.mean(r, axis=1, keepdims=True)
        s = lax.rsqrt(jnp.mean(c * c, axis=1, keepdims=True) + 1e-05)
        n = c * s
        xh1[l, rows] = n
        rs1[l, rows] = jnp.broadcast_to(s, n.shape)
        first = n * norms[l, 0:1] + norms[l, 1:2]
        fb = first.astype(bf16)
        first_b[l, rows] = fb
        h = nn(fb, we[l])
        h2 = h * h
        t = jnp.tanh(0.7978845608028654 * h * (1.0 + 0.044715 * h2))
        act_b = (0.5 * h * (1.0 + t)).astype(bf16)
        act[l, rows] = act_b
        dgelu[l, rows] = 0.5 * (1.0 + t) + 0.5 * h * (1.0 - t * t) * (
            0.7978845608028654 * (1.0 + 3.0 * 0.044715 * h2)
        )
        r = first + nn(act_b, wr[l])
        c = r - jnp.mean(r, axis=1, keepdims=True)
        s = lax.rsqrt(jnp.mean(c * c, axis=1, keepdims=True) + 1e-05)
        n = c * s
        xh2[l, rows] = n
        rs2[l, rows] = jnp.broadcast_to(s, n.shape)
        second = n * norms[l, 2:3] + norms[l, 3:4]
        second = jnp.where(ccol[l, rows] > 0.0, second, 0.0)
        out[rows] = second.astype(bf16).astype(f32)

    def norm_back(d, gain, n, s):
        dn = d * gain
        m1 = jnp.mean(dn, axis=1, keepdims=True)
        m2 = jnp.mean(dn * n, axis=1, keepdims=True)
        return s * (dn - m1 - n * m2)

    def dense_backward(l, first_window, end, grad_out):
        rows = slice(first_window * SLOTS, end * SLOTS)
        d = jnp.where(ccol[l, rows] > 0.0, grad_out[rows], 0.0)
        n2 = xh2[l, rows]
        bias2 = jnp.sum(d, axis=0, keepdims=True)
        gain2 = jnp.sum(d * n2, axis=0, keepdims=True)
        d2 = norm_back(d, norms[l, 2:3], n2, rs2[l, rows])
        b2 = d2.astype(bf16)
        d_br2[rows] = b2
        dh = (nt(b2, wr[l]) * dgelu[l, rows]).astype(bf16)
        d_hid[rows] = dh
        d1 = d2 + nt(dh, we[l])
        n1 = xh1[l, rows]
        bias1 = jnp.sum(d1, axis=0, keepdims=True)
        gain1 = jnp.sum(d1 * n1, axis=0, keepdims=True)
        dr = norm_back(d1, norms[l, 0:1], n1, rs1[l, rows])
        d_res[rows] = dr
        b1 = dr.astype(bf16)
        d_br[rows] = b1
        d_att[rows] = nt(b1, wo[l]).astype(bf16)
        return [gain1, bias1, gain2, bias2]

    def norm_grads(l, parts):
        lines = [sum(lines) for lines in zip(*parts)] + [jnp.zeros((4, D), f32)]
        put(l, "n", jnp.concatenate(lines, axis=0), 8)

    def feed_forward_grads(l):
        put(l, "r", tn(act[l], d_br2[...]), FF)
        d_expand = tn(first_b[l], d_hid[...])
        put(l, "e", jnp.concatenate([d_expand[:, 0:D], d_expand[:, D : 2 * D]], axis=0), FF)

    def attention_backward(l, first_window, end):
        for w in range(first_window, end):
            rows = window_rows(w)
            db = head_blocks(d_att[rows])
            qb = head_blocks(qs[l, rows])
            d_probs = nt(vs[l, rows], db)
            for a, b in TILES:
                dp = d_probs[:, a:b]
                p = probs[l, rows, a:b].astype(f32)
                ds = p * (dp - jnp.sum(dp * p, axis=0, keepdims=True))
                ds_s[rows, a:b] = ds.astype(bf16)
            d_v[rows] = nn(probs[l, rows], db).astype(bf16)
            ds = ds_s[rows]
            d_k[rows] = nn(ds, qb).astype(bf16)
            full = nn(ks[l, rows].T, ds)
            d_q[rows] = (diagonal(full).T * HEAD ** (-0.5)).astype(bf16)

    def attention_grads(l):
        put(l, "o", tn(att[l], d_br[...]), D)
        put(l, "q", tn(mi[l], d_q[...]), D)
        put(l, "k", tn(mi[l], d_k[...]), D)
        put(l, "v", tn(xt[l], d_v[...]), D)
        d_pos = jnp.zeros((SLOTS, D), f32)
        for part, columns in ((d_q, slice(0, D)), (d_k, slice(D, 2 * D))):
            total = part[0:SLOTS].astype(f32)
            for w in range(1, windows):
                total = total + part[window_rows(w)].astype(f32)
            high = total.astype(bf16)
            low = (total - high.astype(f32)).astype(bf16)
            d_pos = d_pos + nt(high, wa[l, :, columns]) + nt(low, wa[l, :, columns])
        put(l, "p", d_pos, SLOTS)

    def input_gradient(l, first_window, end, out):
        rows = slice(first_window * SLOTS, end * SLOTS)
        d = nt(d_q[rows], wa[l, :, 0:D]) + nt(d_k[rows], wa[l, :, D : 2 * D])
        out[rows] = d_res[rows] + d + nt(d_v[rows], wa[l, :, 2 * D : 3 * D])

    def lower(l):
        wa[l] = attend_w[l].astype(bf16)
        wo[l] = output_w[l].astype(bf16)
        we[l] = expand_w[l].astype(bf16)
        wr[l] = reduce_w[l].astype(bf16)

    def to_windows(source, target, chosen):
        for w in chosen:
            for r in range(WIN):
                a = w * SLOTS + r * WIN
                target[a : a + WIN] = source[r * stride + w * WIN : r * stride + (w + 1) * WIN]

    def wrap_ends(field, rows):
        for r in rows:
            field[r * stride + cols : r * stride + cols + hw] = field[r * stride : r * stride + hw]

    def wrap_starts(field, rows):
        for r in rows:
            field[r * stride : r * stride + hw] = field[r * stride + cols : r * stride + cols + hw]

    def to_shifted(source, target, chosen, rows):
        for w in chosen:
            for r in rows:
                a = w * SLOTS + r * WIN
                b = r * stride + w * WIN + hw
                target[a : a + WIN] = source[b : b + WIN]

    def from_shifted(source, source_rows, field, first_row, chosen):
        for w in chosen:
            for r in range(hw):
                a = w * source_rows + r * WIN
                b = (r + first_row) * stride + w * WIN + hw
                field[b : b + WIN] = source[a : a + WIN]

    every = range(windows)
    top, bottom = range(hw), range(hw, WIN)

    loads[0].wait()
    for r in range(WIN):
        field_a[r * stride : r * stride + cols] = feat[r].astype(f32)
    to_windows(field_a, wide_a, every)
    xt[0] = wide_a[...].astype(bf16)
    loads[1].wait()
    csend[...] = jnp.zeros((16, 128), f32)
    for r in range(WIN):
        csend[r : r + 1, 0:cols] = codes_v[r].astype(f32)
    code_tables(0, csend[...])
    for i in range(2, 8):
        loads[i].wait()
    lower(0)
    halo_copies = []
    for i, (a, b) in enumerate(FORWARD_ZERO):
        layer_forward(0, a, b, wide_b)
        for w in range(a, b):
            hsend[w] = wide_b[w * SLOTS : w * SLOTS + hs].astype(bf16)
        if i == 0:
            pl.semaphore_wait(barrier, len(peers))
            codes_copy = remote(csend, crecv, 0, (gi, prev))
            codes_copy.start()
            cot_copy = remote(cot_in.at[pl.ds(0, hw)], grecv, 1, (gi, prev))
            cot_copy.start()
        halo_copies.append(remote(hsend.at[a:b], hrecv.at[a:b], 3 + i, (gi, prev)))
        halo_copies[-1].start()
        if i == 0:
            for load in state_loads:
                load.start()
            lower(1)

    for w in every:
        for r in top:
            a = w * SLOTS + (r + hw) * WIN
            field_b[r * stride + w * WIN : r * stride + (w + 1) * WIN] = wide_b[a : a + WIN]
    wrap_ends(field_b, top)
    to_shifted(field_b, wide_c, every, top)
    codes_copy.wait()
    own = csend[...]
    other = crecv[...]
    table = jnp.concatenate([own[hw:WIN], other[0:hw], jnp.zeros((4, 128), f32)], axis=0)
    table = jnp.concatenate(
        [table[:, hw:cols], table[:, 0:hw], jnp.zeros((16, 128 - cols), f32)], axis=1
    )
    code_tables(1, table)

    arrived = 0
    for a, b in FORWARD_ONE:
        for i, (c, e) in enumerate(FORWARD_ZERO):
            if i >= arrived and c <= b % windows + (windows if b == windows else 0):
                halo_copies[i].wait()
                arrived += 1
                for w in range(c, e):
                    wide_d[w * hs : (w + 1) * hs] = hrecv[w].astype(f32)
                    for r in top:
                        x = w * hs + r * WIN
                        y = (r + hw) * stride + w * WIN
                        field_b[y : y + WIN] = wide_d[x : x + WIN]
                if c == 0:
                    wrap_ends(field_b, bottom)
        to_shifted(field_b, wide_c, range(a, b), bottom)
        rows = slice(a * SLOTS, b * SLOTS)
        xt[1, rows] = wide_c[rows].astype(bf16)
        layer_forward(1, a, b, wide_e)

    for w in every:
        osend[w] = wide_e[w * SLOTS + hs : (w + 1) * SLOTS].astype(bf16)
    out_copy = remote(osend, orecv, 2, (gi, nxt))
    out_copy.start()

    loads[8].wait()
    cot_copy.wait()
    for r in top:
        field_c[r * stride : r * stride + cols] = cot[r + hw].astype(f32)
        field_c[(r + hw) * stride : (r + hw) * stride + cols] = grecv[r].astype(f32)
    wrap_ends(field_c, range(WIN))
    to_shifted(field_c, wide_f, every, range(WIN))
    parts = []
    back_copies = []
    for i, (a, b) in enumerate(BACKWARD_ONE):
        parts.append(dense_backward(1, a, b, wide_f))
        attention_backward(1, a, b)
        input_gradient(1, a, b, wide_g)
        for w in range(a, b):
            bsend[w] = wide_g[w * SLOTS + hs : (w + 1) * SLOTS].astype(bf16)
        back_copies.append(remote(bsend.at[a:b], brecv.at[a:b], 6 + i, (gi, nxt)))
        back_copies[-1].start()
        from_shifted(wide_g, SLOTS, field_d, hw, range(a, b))
    wrap_starts(field_d, bottom)
    norm_grads(1, parts)
    feed_forward_grads(1)
    attention_grads(1)
    totals[0].to_sibling()

    parts = []
    arrived = 0
    for i, ranges in enumerate(BACKWARD_ZERO):
        for j, (c, e) in enumerate(BACKWARD_ONE):
            if j >= arrived and (i == len(BACKWARD_ZERO) - 1 or c < ranges[0][1]):
                back_copies[j].wait()
                arrived += 1
                for w in range(c, e):
                    wide_d[w * hs : (w + 1) * hs] = brecv[w].astype(f32)
                from_shifted(wide_d, hs, field_d, 0, range(c, e))
                if e == windows:
                    wrap_starts(field_d, top)
        if i == 0:
            totals[0].to_chips()
        for a, b in ranges:
            to_windows(field_d, wide_h, range(a, b))
            rows = slice(a * SLOTS, b * SLOTS)
            wide_h[rows] = wide_h[rows].astype(bf16).astype(f32)
            parts.append(dense_backward(0, a, b, wide_h))
        if i == len(BACKWARD_ZERO) - 1:
            feed_forward_grads(0)
            totals[1].to_sibling()
        for a, b in ranges:
            attention_backward(0, a, b)
    norm_grads(0, parts)
    attention_grads(0)
    totals[2].to_sibling()
    totals[1].to_chips()
    totals[2].to_chips()
    totals[0].spread()
    input_gradient(0, 0, windows, wide_a)
    totals[1].spread()
    for w in every:
        for r in range(WIN):
            a = w * SLOTS + r * WIN
            field_a[r * stride + w * WIN : r * stride + (w + 1) * WIN] = wide_a[a : a + WIN]
    for r in range(WIN):
        input_v[r] = field_a[r * stride : r * stride + cols]
    out_copy.wait()
    for w in every:
        wide_d[w * hs : (w + 1) * hs] = orecv[w].astype(f32)
    from_shifted(wide_d, hs, field_c, 0, every)
    from_shifted(wide_e, SLOTS, field_c, hw, every)
    wrap_starts(field_c, range(WIN))
    for r in range(WIN):
        block_v[r] = field_c[r * stride : r * stride + cols].astype(bf16)
    totals[2].spread()
    totals[0].share()
    totals[1].share()
    totals[2].share()
    for load in state_loads:
        load.wait()
    for total in totals:
        total.done()


def main_call(strips, windows, cols, n_grid):
    T = windows * SLOTS
    hw = WIN // 2
    chips = n_grid * strips // 2
    vm = pltpu.VMEM
    hs = hw * WIN
    scratch = [
        vm((WIN, cols, D), bf16),
        vm((WIN, 1, cols), jnp.int32),
        vm((WIN, cols, D), bf16),
        vm((2, D, 3 * D), bf16),
        vm((2, D, D), bf16),
        vm((2, D, FF), bf16),
        vm((2, FF, D), bf16),
        vm((2, T, D), bf16),
        vm((2, T, D), bf16),
        vm((2, T, D), bf16),
        vm((2, T, D), bf16),
        vm((2, T, D), bf16),
        vm((2, T, LANES), bf16),
        vm((2, T, D), bf16),
        vm((2, T, D), bf16),
        vm((2, T, D), f32),
        vm((2, T, D), f32),
        vm((2, T, FF), bf16),
        vm((2, T, FF), f32),
        vm((2, T, D), f32),
        vm((2, T, D), f32),
        vm((2, windows, 1, LANES), f32),
        vm((2, T, D), f32),
        vm((128, LANES), f32),
        *[vm((WIN * (cols + 8), D), f32) for _ in range(4)],
        *[vm((T, D), f32) for _ in range(8)],
        vm((2, SLOTS, LANES), f32),
        vm((T, D), bf16),
        vm((T, FF), bf16),
        vm((T, D), bf16),
        vm((T, D), bf16),
        vm((T, D), f32),
        vm((T, LANES), bf16),
        vm((T, D), bf16),
        vm((T, D), bf16),
        vm((T, D), bf16),
        vm((16, 128), f32),
        vm((16, 128), f32),
        vm((windows, hs, D), bf16),
        vm((windows, hs, D), bf16),
        vm((windows, hs, D), bf16),
        vm((windows, hs, D), bf16),
        vm((hw, cols, D), bf16),
        vm((windows, hs, D), bf16),
        vm((windows, hs, D), bf16),
    ]
    outs = []
    for rows in SET_ROWS:
        c = chunk_rows(rows, 2 * chips)
        scratch += [
            vm((2 * chips * c, D), f32),
            vm((chips, c, D), bf16),
            vm((chips, c, D), bf16),
            vm((chips, c, D), bf16),
            vm((chips, c, D), bf16),
        ]
        outs.append(vm((2, chips, c, D), bf16))
    copies = COPIES + 3 * 2 * chips
    scratch += [pltpu.SemaphoreType.DMA((n,)) for n in (copies, copies, 9, 12)]
    params = [(2, D, 3 * D), (2, D, D), (2, D, FF), (2, FF, D), (2, SLOTS, D), (2, 4, D)]
    outs += [vm(shape, f32) for shape in params * 3]
    near = pl.BlockSpec(memory_space=pltpu.VMEM)
    far = pl.BlockSpec(memory_space=pl.ANY)
    return pl.pallas_call(
        functools.partial(main_kernel, strips, windows, n_grid),
        out_shape=(
            vm((WIN, cols, D), bf16),
            vm((WIN, cols, D), f32),
            *outs,
        ),
        in_specs=[far] * 21,
        out_specs=(near,) * 23,
        scratch_shapes=scratch,
        compiler_params=pltpu.CompilerParams(
            collective_id=0, has_side_effects=True, vmem_limit_bytes=40 * 1024 * 1024
        ),
    )


def lamb_kernel(*refs):
    grads_near = refs[0:3]
    block_near, input_near = refs[3:5]
    states = refs[5:23]
    block_out, input_out = refs[23:25]
    results_far = refs[25:43]
    clip_out, norms_out = refs[43:45]
    results = refs[45:63]
    out_sem, cell_sem = refs[63:65]
    cells = [
        pltpu.make_async_copy(block_near, block_out, cell_sem.at[0]),
        pltpu.make_async_copy(input_near, input_out, cell_sem.at[1]),
    ]
    for copy in cells:
        copy.start()
    stores = [
        pltpu.make_async_copy(results[i], results_far[i], out_sem.at[i]) for i in range(18)
    ]
    grads = [g[...].astype(f32).reshape(-1, D) for g in grads_near]
    clip_norm = jnp.sqrt(sum(jnp.sum(g * g, keepdims=True) for g in grads))
    clip_out[...] = clip_norm
    factor = clip_bound / jnp.maximum(clip_norm, clip_bound)
    fix_one = 1.0 / (1.0 - beta_one**STEP)
    fix_two = 1.0 / (1.0 - beta_two**STEP)

    def grad_rows(l, name, start, rows):
        if l == 1:
            number, table = 0, L1
        elif name in L0_FF:
            number, table = 1, L0_FF
        else:
            number, table = 2, L0_REST
        return grads[number][table[name] + start : table[name] + start + rows]

    def step(index, where, grad, decay):
        grad = grad * factor
        old = states[index][where]
        moment = beta_one * states[6 + index][where] + (1.0 - beta_one) * grad
        square = beta_two * states[12 + index][where] + (1.0 - beta_two) * grad * grad
        results[6 + index][where] = moment
        results[12 + index][where] = square
        direction = moment * fix_one / (jnp.sqrt(square * fix_two) + epsilon)
        if decay:
            direction = direction + weight_decay * old
        return old, direction

    found = {}
    for index, names, height in (
        (0, "qkv", D),
        (1, "o", D),
        (2, "ee", D),
        (3, "r", FF),
        (4, "p", SLOTS),
    ):
        for l in range(2):
            parts = []
            for b, name in enumerate(names):
                where = (l, slice(None), slice(b * D, (b + 1) * D))
                grad = grad_rows(l, name, b * D if name == "e" else 0, height)
                parts.append((where,) + step(index, where, grad, True))
            weight_norm = jnp.sqrt(sum(jnp.sum(old * old, keepdims=True) for _, old, _ in parts))
            step_norm = jnp.sqrt(sum(jnp.sum(d * d, keepdims=True) for _, _, d in parts))
            scale = learn_rate * weight_norm / (step_norm + epsilon)
            for where, old, direction in parts:
                results[index][where] = old - scale * direction
            found[l, index] = (weight_norm, step_norm)
        for kind in range(3):
            stores[6 * kind + index].start()
    for l in range(2):
        old, direction = step(5, (l,), grad_rows(l, "n", 0, 4), False)
        weight_norm = jnp.sqrt(jnp.sum(old * old, axis=1, keepdims=True))
        step_norm = jnp.sqrt(jnp.sum(direction * direction, axis=1, keepdims=True))
        results[5][l] = old - learn_rate * weight_norm / (step_norm + epsilon) * direction
        for r in range(4):
            found[l, 5 + r] = (weight_norm[r : r + 1], step_norm[r : r + 1])
        row = lax.broadcasted_iota(jnp.int32, (2, 9), 0)
        lane = lax.broadcasted_iota(jnp.int32, (2, 9), 1)
        table = jnp.zeros((2, 9), f32)
        for t in range(9):
            for j in range(2):
                value = jnp.broadcast_to(found[l, t][j], (2, 9))
                table = jnp.where((row == j) & (lane == t), value, table)
        norms_out[l] = table
    for kind in range(3):
        stores[6 * kind + 5].start()
    for copy in stores + cells:
        copy.wait()


def lamb_call(grads, block_output, input_grad, states):
    whole = pl.BlockSpec(memory_space=pltpu.VMEM)
    far = pl.BlockSpec(memory_space=pl.ANY)
    like = lambda a: jax.ShapeDtypeStruct(a.shape, a.dtype)
    out = [like(block_output), like(input_grad)]
    out += [like(a) for a in states]
    out += [jax.ShapeDtypeStruct((1, 1), f32), jax.ShapeDtypeStruct((2, 2, 9), f32)]
    near = [pltpu.VMEM(a.shape, a.dtype) for a in states]
    return pl.pallas_call(
        lamb_kernel,
        out_shape=out,
        in_specs=[whole] * 23,
        out_specs=[far] * 20 + [whole] * 2,
        scratch_shapes=near + [pltpu.SemaphoreType.DMA((n,)) for n in (18, 2)],
        compiler_params=pltpu.CompilerParams(vmem_limit_bytes=32 * 1024 * 1024),
    )(*grads, block_output, input_grad, *states)


def body(mesh, features, cell_frame, cotangent, *rest):
    cols = features.shape[2]
    call = main_call(mesh.shape["strip"], cols // WIN, cols, mesh.shape["grid"])
    cell_frame = cell_frame.reshape(WIN, 1, cols)
    held = [
        pltpu.with_memory_space_constraint(a, pltpu.HBM)
        for a in (features[0], cell_frame, cotangent[0], *rest)
    ]
    found = call(*held)
    out = lamb_call(found[2:5], found[0], found[1], found[5:23])
    norms = jnp.swapaxes(out[21], 1, 2)
    return (out[0][None], out[1][None], *out[2:20], out[20].reshape(()), norms)


def solution(mesh):
    cells = P("grid", "strip", None, None)
    return jax.shard_map(
        functools.partial(body, mesh),
        mesh=mesh,
        in_specs=(cells, P("grid", "strip", None), cells) + (P(),) * 18,
        out_specs=(cells, cells) + (P(),) * 20,
        check_vma=False,
    )
```

time: 64.2 us -> 53.6 us (0.83)
  Pallas kernels: 63.2 us -> 52.6 us
    pallas_call x2, Pallas kernels: 63.2 us -> 52.6 us  [the longest x1 48.1 us: body(): found = call(*held)]
where the time goes in v2:
time: 53.6 us; the launch traced here: 53.5 us
  Pallas kernels  52.6 us (98%)
  between operations  0.84 us (2%)
    pallas_call x1, Pallas kernels, body(): found = call(*held)  48.1 us
    pallas_call x1, Pallas kernels, lamb_call(): pl.pallas_call(lamb_kernel, out_shape=out, in_specs=[whole] * 23, out_spe...  4.54 us

profile of v2, /device:TPU:0, one launch (start us, length us, event | category | flops | bytes accessed | tf_op | source)
XLA Modules:
  0.0 53.5 jit_solution(12750314805540469048)
XLA Ops:
  0.7 48.1 %shard_map.372 = (bf16[12,72,128]{2,1,0:T(8,128)(2,1)S(1)}, f32[12,72,128]{2,1,0:T(8,128)S(1)}, bf16[2,16,40,128]{3,2,1,0:T(8,128)(2,1)S(1)}, bf16[2,16,16,128]{...) custom-call(bf16[12,72,128]{2,1,0:T(8,128)(2,1)} %bitcast.7, ...), custom_call_target="tpu_custom_call" | custom-call | tf_op jit(solution)/shard_map/pallas_call | solution.py:846
  48.8 4.5 %shard_map.373 = (bf16[12,72,128]{2,1,0:T(8,128)(2,1)}, f32[12,72,128]{2,1,0:T(8,128)}, f32[2,128,384]{2,1,0:T(8,128)}, f32[2,128,128]{2,1,0:T(8,128)}, f32[2,12...) custom-call(bf16[2,16,40,128]{3,2,1,0:T(8,128)(2,1)S(1)} %get-tuple-, ...), custom_call_target="tpu_custom_call" | custom-call | tf_op jit(solution)/shard_map/pallas_call | solution.py:828

commit v3 on v2

--- a/solution.py
+++ b/solution.py
@@ -32,13 +32,13 @@
 L0_REST = dict(q=0, k=128, v=256, o=384, p=512, n=656)
 SET_ROWS = (1176, 512, 664)
 
-FORWARD_ZERO = ((0, 2), (2, 4), (4, 6))
-FORWARD_ONE = ((0, 3), (3, 6))
-BACKWARD_ONE = ((0, 2), (2, 4), (4, 6))
-BACKWARD_ZERO = (((1, 4),), ((4, 6), (0, 1)))
+FORWARD_ZERO = ((0, 6),)
+FORWARD_ONE = ((0, 6),)
+BACKWARD_ONE = ((0, 6),)
+BACKWARD_ZERO = (((0, 6),),)
 COPIES = 9
 
-TILES = tuple((a, a + 128) for a in range(0, LANES, 128))
+TILES = tuple((a, min(a + 256, LANES)) for a in range(0, LANES, 256))
 
 
 def nt(a, b):
@@ -60,14 +60,6 @@
         keep = (lane >= h * HEAD) & (lane < (h + 1) * HEAD)
         parts.append(jnp.where(keep, block, jnp.zeros_like(block)))
     return jnp.concatenate(parts, axis=0)
-
-
-def merged(full):
-    lane = lax.broadcasted_iota(jnp.int32, (SLOTS, D), 1)
-    block = full[0:SLOTS]
-    for h in range(1, HEADS):
-        block = jnp.where(lane >= h * HEAD, full[h * SLOTS : (h + 1) * SLOTS], block)
-    return block
 
 
 def diagonal(full):
@@ -241,7 +233,7 @@
             ]
             self.out = outs[2 + number]
             self.c = chunk_rows(SET_ROWS[number], 2 * chips)
-            self.sem = COPIES + number * 2 * chips
+            self.sem = COPIES + number * 4
 
         def rows(self, half, j):
             return pl.ds(pl.multiple_of((half * chips + j) * self.c, 8), self.c)
@@ -260,32 +252,28 @@
             for j in range(chips):
                 both = self.g[self.rows(core, j)] + self.r1[j].astype(f32)
                 self.s2[j] = both.astype(bf16)
-            self.copies = []
-            for i, (number, device) in enumerate(others):
-                copy = remote(self.s2.at[number], self.r2.at[chip], self.sem + 1 + i, device)
-                copy.start()
-                self.copies.append(copy)
+            for number, device in others:
+                remote(self.s2.at[number], self.r2.at[chip], self.sem + 1, device).start()
             self.r2[chip] = self.s2[chip]
 
+        def all_arrived(self, buffer, index):
+            bytes_of = buffer.at[pl.ds(0, chips - 1)]
+            remote(bytes_of, bytes_of, index, (gi, sib)).wait()
+
         def spread(self):
-            for copy in self.copies:
-                copy.wait()
+            self.all_arrived(self.r2, self.sem + 1)
             total = self.r2[0].astype(f32)
             for j in range(1, chips):
                 total = total + self.r2[j].astype(f32)
             self.out[core, chip] = total.astype(bf16)
-            self.copies = []
-            for i, (number, device) in enumerate(others):
-                mine = self.out.at[core, chip]
-                copy = remote(mine, mine, self.sem + chips + i, device)
-                copy.start()
-                self.copies.append(copy)
+            mine = self.out.at[core, chip]
+            for number, device in others:
+                remote(mine, mine, self.sem + 2, device).start()
 
         def share(self):
-            for copy in self.copies:
-                copy.wait()
+            self.all_arrived(self.r2, self.sem + 2)
             mine = self.out.at[core]
-            self.last = remote(mine, mine, self.sem + 2 * chips - 1, (gi, sib))
+            self.last = remote(mine, mine, self.sem + 3, (gi, sib))
             self.last.start()
 
         def done(self):
@@ -329,6 +317,16 @@
     def window_rows(w):
         return slice(w * SLOTS, (w + 1) * SLOTS)
 
+    def in_turn(chosen, before, middle, after):
+        before(chosen[0])
+        for i, w in enumerate(chosen):
+            if i + 1 < len(chosen):
+                before(chosen[i + 1])
+            middle(w)
+            if i > 0:
+                after(chosen[i - 1])
+        after(chosen[-1])
+
     def layer_forward(l, first_window, end, out):
         rows = slice(first_window * SLOTS, end * SLOTS)
         x = xt[l, rows]
@@ -340,19 +338,27 @@
         ks[l, rows] = qk[:, D : 2 * D].astype(bf16)
         vs[l, rows] = nn(x, wa[l, :, 2 * D : 3 * D]).astype(bf16)
 
-        for w in range(first_window, end):
+        def scores_of(w):
             one = window_rows(w)
-            qb = head_blocks(qs[l, one])
-            scores_s[w % 2] = nt(ks[l, one], qb)
+            scores_s[w] = nt(ks[l, one], head_blocks(qs[l, one]))
+
+        def soften(w):
+            one = window_rows(w)
             cc = ccol[l, one]
             cr = crow[l, w]
             for a, b in TILES:
-                scores = jnp.where(cc == cr[:, a:b], scores_s[w % 2, :, a:b], -1000000000.0)
+                same = jnp.concatenate([cc] * ((b - a) // 128), axis=1) == cr[:, a:b]
+                scores = jnp.where(same, scores_s[w, :, a:b], -1000000000.0)
                 top = jnp.max(scores, axis=0, keepdims=True)
                 weights = jnp.exp(scores - top)
                 total = jnp.sum(weights, axis=0, keepdims=True)
                 probs[l, one, a:b] = (weights * (1.0 / total)).astype(bf16)
-            att[l, one] = merged(tn(probs[l, one], vs[l, one])).astype(bf16)
+
+        def mix(w):
+            one = window_rows(w)
+            att[l, one] = diagonal(nn(vs[l, one].T, probs[l, one])).T.astype(bf16)
+
+        in_turn(range(first_window, end), scores_of, soften, mix)
 
         r = xt[l, rows].astype(f32) + nn(att[l, rows], wo[l])
         c = r - jnp.mean(r, axis=1, keepdims=True)
@@ -418,22 +424,29 @@
         d_expand = tn(first_b[l], d_hid[...])
         put(l, "e", jnp.concatenate([d_expand[:, 0:D], d_expand[:, D : 2 * D]], axis=0), FF)
 
-    def attention_backward(l, first_window, end):
-        for w in range(first_window, end):
+    def attention_backward(l, chosen):
+        def d_probs_of(w):
             rows = window_rows(w)
             db = head_blocks(d_att[rows])
-            qb = head_blocks(qs[l, rows])
-            d_probs = nt(vs[l, rows], db)
+            d_v[rows] = nn(probs[l, rows], db).astype(bf16)
+            scores_s[w] = nt(vs[l, rows], db)
+
+        def d_soften(w):
+            rows = window_rows(w)
             for a, b in TILES:
-                dp = d_probs[:, a:b]
+                dp = scores_s[w, :, a:b]
                 p = probs[l, rows, a:b].astype(f32)
                 ds = p * (dp - jnp.sum(dp * p, axis=0, keepdims=True))
                 ds_s[rows, a:b] = ds.astype(bf16)
-            d_v[rows] = nn(probs[l, rows], db).astype(bf16)
+
+        def d_mix(w):
+            rows = window_rows(w)
             ds = ds_s[rows]
-            d_k[rows] = nn(ds, qb).astype(bf16)
+            d_k[rows] = nn(ds, head_blocks(qs[l, rows])).astype(bf16)
             full = nn(ks[l, rows].T, ds)
             d_q[rows] = (diagonal(full).T * HEAD ** (-0.5)).astype(bf16)
+
+        in_turn(chosen, d_probs_of, d_soften, d_mix)
 
     def attention_grads(l):
         put(l, "o", tn(att[l], d_br[...]), D)
@@ -514,8 +527,6 @@
             pl.semaphore_wait(barrier, len(peers))
             codes_copy = remote(csend, crecv, 0, (gi, prev))
             codes_copy.start()
-            cot_copy = remote(cot_in.at[pl.ds(0, hw)], grecv, 1, (gi, prev))
-            cot_copy.start()
         halo_copies.append(remote(hsend.at[a:b], hrecv.at[a:b], 3 + i, (gi, prev)))
         halo_copies[-1].start()
         if i == 0:
@@ -529,6 +540,11 @@
             field_b[r * stride + w * WIN : r * stride + (w + 1) * WIN] = wide_b[a : a + WIN]
     wrap_ends(field_b, top)
     to_shifted(field_b, wide_c, every, top)
+    loads[8].wait()
+    for r in top:
+        field_c[r * stride : r * stride + cols] = cot[r + hw].astype(f32)
+    wrap_ends(field_c, top)
+    to_shifted(field_c, wide_f, every, top)
     codes_copy.wait()
     own = csend[...]
     other = crecv[...]
@@ -537,7 +553,6 @@
         [table[:, hw:cols], table[:, 0:hw], jnp.zeros((16, 128 - cols), f32)], axis=1
     )
     code_tables(1, table)
-
     arrived = 0
     for a, b in FORWARD_ONE:
         for i, (c, e) in enumerate(FORWARD_ZERO):
@@ -552,6 +567,9 @@
                         field_b[y : y + WIN] = wide_d[x : x + WIN]
                 if c == 0:
                     wrap_ends(field_b, bottom)
+        if arrived == len(halo_copies):
+            cot_copy = remote(cot_in.at[pl.ds(0, hw)], grecv, 1, (gi, prev))
+            cot_copy.start()
         to_shifted(field_b, wide_c, range(a, b), bottom)
         rows = slice(a * SLOTS, b * SLOTS)
         xt[1, rows] = wide_c[rows].astype(bf16)
@@ -562,18 +580,16 @@
     out_copy = remote(osend, orecv, 2, (gi, nxt))
     out_copy.start()
 
-    loads[8].wait()
     cot_copy.wait()
     for r in top:
-        field_c[r * stride : r * stride + cols] = cot[r + hw].astype(f32)
         field_c[(r + hw) * stride : (r + hw) * stride + cols] = grecv[r].astype(f32)
-    wrap_ends(field_c, range(WIN))
-    to_shifted(field_c, wide_f, every, range(WIN))
+    wrap_ends(field_c, bottom)
+    to_shifted(field_c, wide_f, every, bottom)
     parts = []
     back_copies = []
     for i, (a, b) in enumerate(BACKWARD_ONE):
         parts.append(dense_backward(1, a, b, wide_f))
-        attention_backward(1, a, b)
+        attention_backward(1, range(a, b))
         input_gradient(1, a, b, wide_g)
         for w in range(a, b):
             bsend[w] = wide_g[w * SLOTS + hs : (w + 1) * SLOTS].astype(bf16)
@@ -608,16 +624,14 @@
         if i == len(BACKWARD_ZERO) - 1:
             feed_forward_grads(0)
             totals[1].to_sibling()
-        for a, b in ranges:
-            attention_backward(0, a, b)
+        attention_backward(0, [w for a, b in ranges for w in range(a, b)])
     norm_grads(0, parts)
     attention_grads(0)
     totals[2].to_sibling()
+    totals[0].spread()
+    totals[2].to_chips()
     totals[1].to_chips()
-    totals[2].to_chips()
-    totals[0].spread()
     input_gradient(0, 0, windows, wide_a)
-    totals[1].spread()
     for w in every:
         for r in range(WIN):
             a = w * SLOTS + r * WIN
@@ -633,9 +647,10 @@
     for r in range(WIN):
         block_v[r] = field_c[r * stride : r * stride + cols].astype(bf16)
     totals[2].spread()
+    totals[1].spread()
     totals[0].share()
+    totals[2].share()
     totals[1].share()
-    totals[2].share()
     for load in state_loads:
         load.wait()
     for total in totals:
@@ -675,7 +690,7 @@
         vm((128, LANES), f32),
         *[vm((WIN * (cols + 8), D), f32) for _ in range(4)],
         *[vm((T, D), f32) for _ in range(8)],
-        vm((2, SLOTS, LANES), f32),
+        vm((windows, SLOTS, LANES), f32),
         vm((T, D), bf16),
         vm((T, FF), bf16),
         vm((T, D), bf16),
@@ -706,7 +721,7 @@
             vm((chips, c, D), bf16),
         ]
         outs.append(vm((2, chips, c, D), bf16))
-    copies = COPIES + 3 * 2 * chips
+    copies = COPIES + 3 * 4
     scratch += [pltpu.SemaphoreType.DMA((n,)) for n in (copies, copies, 9, 12)]
     params = [(2, D, 3 * D), (2, D, D), (2, D, FF), (2, FF, D), (2, SLOTS, D), (2, 4, D)]
     outs += [vm(shape, f32) for shape in params * 3]
@@ -772,30 +787,32 @@
         direction = moment * fix_one / (jnp.sqrt(square * fix_two) + epsilon)
         if decay:
             direction = direction + weight_decay * old
+        results[index][where] = direction
         return old, direction
 
     found = {}
-    for index, names, height in (
-        (0, "qkv", D),
-        (1, "o", D),
-        (2, "ee", D),
-        (3, "r", FF),
-        (4, "p", SLOTS),
-    ):
+    order = ((0, "qkv", D), (2, "ee", D), (3, "r", FF), (4, "p", SLOTS), (1, "o", D))
+    for index, names, height in order:
         for l in range(2):
-            parts = []
+            weight_sum, step_sum = [], []
             for b, name in enumerate(names):
                 where = (l, slice(None), slice(b * D, (b + 1) * D))
                 grad = grad_rows(l, name, b * D if name == "e" else 0, height)
-                parts.append((where,) + step(index, where, grad, True))
-            weight_norm = jnp.sqrt(sum(jnp.sum(old * old, keepdims=True) for _, old, _ in parts))
-            step_norm = jnp.sqrt(sum(jnp.sum(d * d, keepdims=True) for _, _, d in parts))
+                old, direction = step(index, where, grad, True)
+                weight_sum.append(jnp.sum(old * old, axis=0, keepdims=True))
+                step_sum.append(jnp.sum(direction * direction, axis=0, keepdims=True))
+            found[l, index] = tuple(
+                jnp.sqrt(jnp.sum(sum(parts), axis=1, keepdims=True))
+                for parts in (weight_sum, step_sum)
+            )
+        for kind in (1, 2):
+            stores[6 * kind + index].start()
+    for index, names, _ in order:
+        for l in range(2):
+            weight_norm, step_norm = found[l, index]
             scale = learn_rate * weight_norm / (step_norm + epsilon)
-            for where, old, direction in parts:
-                results[index][where] = old - scale * direction
-            found[l, index] = (weight_norm, step_norm)
-        for kind in range(3):
-            stores[6 * kind + index].start()
+            results[index][l] = states[index][l] - scale * results[index][l]
+        stores[index].start()
     for l in range(2):
         old, direction = step(5, (l,), grad_rows(l, "n", 0, 4), False)
         weight_norm = jnp.sqrt(jnp.sum(old * old, axis=1, keepdims=True))

time: 53.6 us -> 47.8 us (0.89)
  Pallas kernels: 52.6 us -> 46.8 us
    pallas_call x1, Pallas kernels: 48.1 us -> 42.8 us  [body(): found = call(*held)]
    pallas_call x1, Pallas kernels: 4.54 us -> 3.94 us  [lamb_call(): pl.pallas_call(lamb_kernel, out_shape=out, in_specs=[whole] * 23, out_spe...]
where the time goes in v3:
time: 47.8 us; the launch traced here: 47.6 us
  Pallas kernels  46.8 us (98%)
  between operations  0.84 us (2%)
    pallas_call x1, Pallas kernels, body(): found = call(*held)  42.8 us
    pallas_call x1, Pallas kernels, lamb_call(): pl.pallas_call(lamb_kernel, out_shape=out, in_specs=[whole] * 23, out_spe...  3.94 us

profile of v3, /device:TPU:0, one launch (start us, length us, event | category | flops | bytes accessed | tf_op | source)
XLA Modules:
  0.0 47.6 jit_solution(7622176577779432586)
XLA Ops:
  0.7 42.8 %shard_map.372 = (bf16[12,72,128]{2,1,0:T(8,128)(2,1)S(1)}, f32[12,72,128]{2,1,0:T(8,128)S(1)}, bf16[2,16,40,128]{3,2,1,0:T(8,128)(2,1)S(1)}, bf16[2,16,16,128]{...) custom-call(bf16[12,72,128]{2,1,0:T(8,128)(2,1)} %bitcast.7, ...), custom_call_target="tpu_custom_call" | custom-call | tf_op jit(solution)/shard_map/pallas_call | solution.py:863
  43.5 3.9 %shard_map.373 = (bf16[12,72,128]{2,1,0:T(8,128)(2,1)}, f32[12,72,128]{2,1,0:T(8,128)}, f32[2,128,384]{2,1,0:T(8,128)}, f32[2,128,128]{2,1,0:T(8,128)}, f32[2,12...) custom-call(bf16[2,16,40,128]{3,2,1,0:T(8,128)(2,1)S(1)} %get-tuple-, ...), custom_call_target="tpu_custom_call" | custom-call | tf_op jit(solution)/shard_map/pallas_call | solution.py:845

commit v4 on v3

--- a/solution.py
+++ b/solution.py
@@ -32,13 +32,18 @@
 L0_REST = dict(q=0, k=128, v=256, o=384, p=512, n=656)
 SET_ROWS = (1176, 512, 664)
 
-FORWARD_ZERO = ((0, 6),)
-FORWARD_ONE = ((0, 6),)
-BACKWARD_ONE = ((0, 6),)
-BACKWARD_ZERO = (((0, 6),),)
-COPIES = 9
-
-TILES = tuple((a, min(a + 256, LANES)) for a in range(0, LANES, 256))
+PARTS = ((0, 80), (80, SLOTS))
+BOTH = (0, 1)
+COPIES = 5
+
+
+def lanes_of(parts):
+    return HEADS * PARTS[parts[0]][0], HEADS * PARTS[parts[-1]][1]
+
+
+def tiles_of(parts):
+    first, end = lanes_of(parts)
+    return [(a, min(a + 256, end)) for a in range(first, end, 256)]
 
 
 def nt(a, b):
@@ -63,9 +68,10 @@
 
 
 def diagonal(full):
+    n = full.shape[1] // HEADS
     return jnp.concatenate(
-        [full[h * HEAD : (h + 1) * HEAD, h * SLOTS : (h + 1) * SLOTS] for h in range(HEADS)], axis=0
-    )
+        [full[h * HEAD : (h + 1) * HEAD, h * n : (h + 1) * n] for h in range(HEADS)], axis=0
+    ).T
 
 
 def chunk_rows(rows, parts):
@@ -144,6 +150,8 @@
     wide_f,
     wide_g,
     wide_h,
+    kept_v,
+    kept_k,
     scores_s,
     d_br2,
     d_hid,
@@ -294,7 +302,11 @@
         low = table.astype(bf16)
         lane = lax.broadcasted_iota(jnp.int32, (16, LANES), 1).astype(f32)
         row = lax.broadcasted_iota(jnp.int32, (16, LANES), 0).astype(f32)
-        slot = lane - SLOTS * jnp.floor((lane + 0.5) * (1.0 / SLOTS))
+        cut, end = PARTS[0][1], PARTS[1][1]
+        lane_b = lane - HEADS * cut
+        slot_a = lane - cut * jnp.floor((lane + 0.5) * (1.0 / cut))
+        slot_b = lane_b - (end - cut) * jnp.floor((lane_b + 0.5) * (1.0 / (end - cut))) + cut
+        slot = jnp.where(lane_b < 0.0, slot_a, slot_b)
         slot_r = jnp.floor((slot + 0.5) * (1.0 / WIN))
         slot_c = slot - WIN * slot_r
         pick_r = (slot_r == row).astype(bf16)
@@ -314,6 +326,8 @@
             value = jnp.sum(chosen, axis=1, keepdims=True)
             ccol[l, w * SLOTS : (w + 1) * SLOTS] = jnp.broadcast_to(value, (SLOTS, 128))
 
+    every = range(windows)
+
     def window_rows(w):
         return slice(w * SLOTS, (w + 1) * SLOTS)
 
@@ -327,26 +341,53 @@
                 after(chosen[i - 1])
         after(chosen[-1])
 
-    def layer_forward(l, first_window, end, out):
-        rows = slice(first_window * SLOTS, end * SLOTS)
-        x = xt[l, rows]
-        places = jnp.concatenate([position[l]] * (end - first_window), axis=0)
-        m = (x.astype(f32) + places).astype(bf16)
-        mi[l, rows] = m
+    def rows_of(w, p):
+        return slice(w * SLOTS + PARTS[p][0], w * SLOTS + PARTS[p][1])
+
+    def take(ref, parts):
+        if parts == BOTH:
+            return ref[...]
+        return jnp.concatenate([ref[rows_of(w, p)] for w in every for p in parts], axis=0)
+
+    def give(ref, parts, value):
+        if parts == BOTH:
+            ref[...] = value
+            return
+        n = value.shape[0] // windows
+        for w in every:
+            ref[rows_of(w, parts[0])] = value[w * n : (w + 1) * n]
+
+    def blocks(ref, w, parts):
+        return jnp.concatenate([head_blocks(ref[rows_of(w, p)]) for p in parts], axis=0)
+
+    def diagonals(full, parts):
+        first, _ = lanes_of(parts)
+        found = []
+        for p in parts:
+            a, b = lanes_of((p,))
+            found.append(diagonal(full[:, a - first : b - first]))
+        return found
+
+    def project(l):
+        x = xt[l]
+        m = (x.astype(f32) + jnp.concatenate([position[l]] * windows, axis=0)).astype(bf16)
+        mi[l] = m
         qk = nn(m, wa[l, :, 0 : 2 * D])
-        qs[l, rows] = (qk[:, 0:D] * HEAD ** (-0.5)).astype(bf16)
-        ks[l, rows] = qk[:, D : 2 * D].astype(bf16)
-        vs[l, rows] = nn(x, wa[l, :, 2 * D : 3 * D]).astype(bf16)
+        qs[l] = (qk[:, 0:D] * HEAD ** (-0.5)).astype(bf16)
+        ks[l] = qk[:, D : 2 * D].astype(bf16)
+        vs[l] = nn(x, wa[l, :, 2 * D : 3 * D]).astype(bf16)
+
+    def attend(l, parts):
+        first, end = lanes_of(parts)
 
         def scores_of(w):
-            one = window_rows(w)
-            scores_s[w] = nt(ks[l, one], head_blocks(qs[l, one]))
+            scores_s[w, :, first:end] = nt(ks[l, window_rows(w)], blocks(qs.at[l], w, parts))
 
         def soften(w):
             one = window_rows(w)
             cc = ccol[l, one]
             cr = crow[l, w]
-            for a, b in TILES:
+            for a, b in tiles_of(parts):
                 same = jnp.concatenate([cc] * ((b - a) // 128), axis=1) == cr[:, a:b]
                 scores = jnp.where(same, scores_s[w, :, a:b], -1000000000.0)
                 top = jnp.max(scores, axis=0, keepdims=True)
@@ -356,36 +397,38 @@
 
         def mix(w):
             one = window_rows(w)
-            att[l, one] = diagonal(nn(vs[l, one].T, probs[l, one])).T.astype(bf16)
-
-        in_turn(range(first_window, end), scores_of, soften, mix)
-
-        r = xt[l, rows].astype(f32) + nn(att[l, rows], wo[l])
+            full = nn(vs[l, one].T, probs[l, one, first:end])
+            for p, value in zip(parts, diagonals(full, parts)):
+                att[l, rows_of(w, p)] = value.astype(bf16)
+
+        in_turn(every, scores_of, soften, mix)
+
+    def feed_forward(l, parts, out):
+        r = take(xt.at[l], parts).astype(f32) + nn(take(att.at[l], parts), wo[l])
         c = r - jnp.mean(r, axis=1, keepdims=True)
         s = lax.rsqrt(jnp.mean(c * c, axis=1, keepdims=True) + 1e-05)
         n = c * s
-        xh1[l, rows] = n
-        rs1[l, rows] = jnp.broadcast_to(s, n.shape)
+        give(xh1.at[l], parts, n)
+        give(rs1.at[l], parts, jnp.broadcast_to(s, n.shape))
         first = n * norms[l, 0:1] + norms[l, 1:2]
         fb = first.astype(bf16)
-        first_b[l, rows] = fb
+        give(first_b.at[l], parts, fb)
         h = nn(fb, we[l])
         h2 = h * h
         t = jnp.tanh(0.7978845608028654 * h * (1.0 + 0.044715 * h2))
         act_b = (0.5 * h * (1.0 + t)).astype(bf16)
-        act[l, rows] = act_b
-        dgelu[l, rows] = 0.5 * (1.0 + t) + 0.5 * h * (1.0 - t * t) * (
-            0.7978845608028654 * (1.0 + 3.0 * 0.044715 * h2)
-        )
+        give(act.at[l], parts, act_b)
+        slope = 0.7978845608028654 * (1.0 + 3.0 * 0.044715 * h2)
+        give(dgelu.at[l], parts, 0.5 * (1.0 + t) + 0.5 * h * (1.0 - t * t) * slope)
         r = first + nn(act_b, wr[l])
         c = r - jnp.mean(r, axis=1, keepdims=True)
         s = lax.rsqrt(jnp.mean(c * c, axis=1, keepdims=True) + 1e-05)
         n = c * s
-        xh2[l, rows] = n
-        rs2[l, rows] = jnp.broadcast_to(s, n.shape)
+        give(xh2.at[l], parts, n)
+        give(rs2.at[l], parts, jnp.broadcast_to(s, n.shape))
         second = n * norms[l, 2:3] + norms[l, 3:4]
-        second = jnp.where(ccol[l, rows] > 0.0, second, 0.0)
-        out[rows] = second.astype(bf16).astype(f32)
+        second = jnp.where(take(ccol.at[l], parts) > 0.0, second, 0.0)
+        give(out, parts, second.astype(bf16).astype(f32))
 
     def norm_back(d, gain, n, s):
         dn = d * gain
@@ -393,26 +436,25 @@
         m2 = jnp.mean(dn * n, axis=1, keepdims=True)
         return s * (dn - m1 - n * m2)
 
-    def dense_backward(l, first_window, end, grad_out):
-        rows = slice(first_window * SLOTS, end * SLOTS)
-        d = jnp.where(ccol[l, rows] > 0.0, grad_out[rows], 0.0)
-        n2 = xh2[l, rows]
+    def dense_backward(l, parts, grad_out):
+        d = jnp.where(take(ccol.at[l], parts) > 0.0, take(grad_out, parts), 0.0)
+        n2 = take(xh2.at[l], parts)
         bias2 = jnp.sum(d, axis=0, keepdims=True)
         gain2 = jnp.sum(d * n2, axis=0, keepdims=True)
-        d2 = norm_back(d, norms[l, 2:3], n2, rs2[l, rows])
+        d2 = norm_back(d, norms[l, 2:3], n2, take(rs2.at[l], parts))
         b2 = d2.astype(bf16)
-        d_br2[rows] = b2
-        dh = (nt(b2, wr[l]) * dgelu[l, rows]).astype(bf16)
-        d_hid[rows] = dh
+        give(d_br2, parts, b2)
+        dh = (nt(b2, wr[l]) * take(dgelu.at[l], parts)).astype(bf16)
+        give(d_hid, parts, dh)
         d1 = d2 + nt(dh, we[l])
-        n1 = xh1[l, rows]
+        n1 = take(xh1.at[l], parts)
         bias1 = jnp.sum(d1, axis=0, keepdims=True)
         gain1 = jnp.sum(d1 * n1, axis=0, keepdims=True)
-        dr = norm_back(d1, norms[l, 0:1], n1, rs1[l, rows])
-        d_res[rows] = dr
+        dr = norm_back(d1, norms[l, 0:1], n1, take(rs1.at[l], parts))
+        give(d_res, parts, dr)
         b1 = dr.astype(bf16)
-        d_br[rows] = b1
-        d_att[rows] = nt(b1, wo[l]).astype(bf16)
+        give(d_br, parts, b1)
+        give(d_att, parts, nt(b1, wo[l]).astype(bf16))
         return [gain1, bias1, gain2, bias2]
 
     def norm_grads(l, parts):
@@ -424,16 +466,26 @@
         d_expand = tn(first_b[l], d_hid[...])
         put(l, "e", jnp.concatenate([d_expand[:, 0:D], d_expand[:, D : 2 * D]], axis=0), FF)
 
-    def attention_backward(l, chosen):
+    def attention_backward(l, parts, add_to=None, keep=None):
+        first, end = lanes_of(parts)
+
+        def put_rows(which, target, rows, value):
+            if keep is not None:
+                keep[which][rows] = value
+                return
+            if add_to is not None:
+                value = value + add_to[which][rows]
+            target[rows] = value.astype(bf16)
+
         def d_probs_of(w):
             rows = window_rows(w)
-            db = head_blocks(d_att[rows])
-            d_v[rows] = nn(probs[l, rows], db).astype(bf16)
-            scores_s[w] = nt(vs[l, rows], db)
+            db = blocks(d_att, w, parts)
+            put_rows(0, d_v, rows, nn(probs[l, rows, first:end], db))
+            scores_s[w, :, first:end] = nt(vs[l, rows], db)
 
         def d_soften(w):
             rows = window_rows(w)
-            for a, b in TILES:
+            for a, b in tiles_of(parts):
                 dp = scores_s[w, :, a:b]
                 p = probs[l, rows, a:b].astype(f32)
                 ds = p * (dp - jnp.sum(dp * p, axis=0, keepdims=True))
@@ -441,12 +493,13 @@
 
         def d_mix(w):
             rows = window_rows(w)
-            ds = ds_s[rows]
-            d_k[rows] = nn(ds, head_blocks(qs[l, rows])).astype(bf16)
+            ds = ds_s[rows, first:end]
+            put_rows(1, d_k, rows, nn(ds, blocks(qs.at[l], w, parts)))
             full = nn(ks[l, rows].T, ds)
-            d_q[rows] = (diagonal(full).T * HEAD ** (-0.5)).astype(bf16)
-
-        in_turn(chosen, d_probs_of, d_soften, d_mix)
+            for p, value in zip(parts, diagonals(full, parts)):
+                d_q[rows_of(w, p)] = (value * HEAD ** (-0.5)).astype(bf16)
+
+        in_turn(every, d_probs_of, d_soften, d_mix)
 
     def attention_grads(l):
         put(l, "o", tn(att[l], d_br[...]), D)
@@ -463,10 +516,9 @@
             d_pos = d_pos + nt(high, wa[l, :, columns]) + nt(low, wa[l, :, columns])
         put(l, "p", d_pos, SLOTS)
 
-    def input_gradient(l, first_window, end, out):
-        rows = slice(first_window * SLOTS, end * SLOTS)
-        d = nt(d_q[rows], wa[l, :, 0:D]) + nt(d_k[rows], wa[l, :, D : 2 * D])
-        out[rows] = d_res[rows] + d + nt(d_v[rows], wa[l, :, 2 * D : 3 * D])
+    def input_gradient(l, out):
+        d = nt(d_q[...], wa[l, :, 0:D]) + nt(d_k[...], wa[l, :, D : 2 * D])
+        out[...] = d_res[...] + d + nt(d_v[...], wa[l, :, 2 * D : 3 * D])
 
     def lower(l):
         wa[l] = attend_w[l].astype(bf16)
@@ -474,9 +526,9 @@
         we[l] = expand_w[l].astype(bf16)
         wr[l] = reduce_w[l].astype(bf16)
 
-    def to_windows(source, target, chosen):
-        for w in chosen:
-            for r in range(WIN):
+    def to_windows(source, target, rows):
+        for w in every:
+            for r in rows:
                 a = w * SLOTS + r * WIN
                 target[a : a + WIN] = source[r * stride + w * WIN : r * stride + (w + 1) * WIN]
 
@@ -488,27 +540,26 @@
         for r in rows:
             field[r * stride : r * stride + hw] = field[r * stride + cols : r * stride + cols + hw]
 
-    def to_shifted(source, target, chosen, rows):
-        for w in chosen:
+    def to_shifted(source, target, rows):
+        for w in every:
             for r in rows:
                 a = w * SLOTS + r * WIN
                 b = r * stride + w * WIN + hw
                 target[a : a + WIN] = source[b : b + WIN]
 
-    def from_shifted(source, source_rows, field, first_row, chosen):
-        for w in chosen:
+    def from_shifted(source, source_rows, field, first_row):
+        for w in every:
             for r in range(hw):
                 a = w * source_rows + r * WIN
                 b = (r + first_row) * stride + w * WIN + hw
                 field[b : b + WIN] = source[a : a + WIN]
 
-    every = range(windows)
     top, bottom = range(hw), range(hw, WIN)
 
     loads[0].wait()
     for r in range(WIN):
         field_a[r * stride : r * stride + cols] = feat[r].astype(f32)
-    to_windows(field_a, wide_a, every)
+    to_windows(field_a, wide_a, range(WIN))
     xt[0] = wide_a[...].astype(bf16)
     loads[1].wait()
     csend[...] = jnp.zeros((16, 128), f32)
@@ -518,33 +569,33 @@
     for i in range(2, 8):
         loads[i].wait()
     lower(0)
-    halo_copies = []
-    for i, (a, b) in enumerate(FORWARD_ZERO):
-        layer_forward(0, a, b, wide_b)
-        for w in range(a, b):
-            hsend[w] = wide_b[w * SLOTS : w * SLOTS + hs].astype(bf16)
-        if i == 0:
-            pl.semaphore_wait(barrier, len(peers))
-            codes_copy = remote(csend, crecv, 0, (gi, prev))
-            codes_copy.start()
-        halo_copies.append(remote(hsend.at[a:b], hrecv.at[a:b], 3 + i, (gi, prev)))
-        halo_copies[-1].start()
-        if i == 0:
-            for load in state_loads:
-                load.start()
-            lower(1)
-
+    project(0)
+    attend(0, (0,))
+    feed_forward(0, (0,), wide_b)
+    for w in every:
+        hsend[w] = wide_b[w * SLOTS : w * SLOTS + hs].astype(bf16)
+    pl.semaphore_wait(barrier, len(peers))
+    codes_copy = remote(csend, crecv, 0, (gi, prev))
+    codes_copy.start()
+    halo_copy = remote(hsend, hrecv, 1, (gi, prev))
+    halo_copy.start()
+    for load in state_loads:
+        load.start()
+
+    attend(0, (1,))
+    feed_forward(0, (1,), wide_b)
+    lower(1)
     for w in every:
         for r in top:
             a = w * SLOTS + (r + hw) * WIN
             field_b[r * stride + w * WIN : r * stride + (w + 1) * WIN] = wide_b[a : a + WIN]
     wrap_ends(field_b, top)
-    to_shifted(field_b, wide_c, every, top)
+    to_shifted(field_b, wide_c, top)
     loads[8].wait()
     for r in top:
         field_c[r * stride : r * stride + cols] = cot[r + hw].astype(f32)
     wrap_ends(field_c, top)
-    to_shifted(field_c, wide_f, every, top)
+    to_shifted(field_c, wide_f, top)
     codes_copy.wait()
     own = csend[...]
     other = crecv[...]
@@ -553,85 +604,71 @@
         [table[:, hw:cols], table[:, 0:hw], jnp.zeros((16, 128 - cols), f32)], axis=1
     )
     code_tables(1, table)
-    arrived = 0
-    for a, b in FORWARD_ONE:
-        for i, (c, e) in enumerate(FORWARD_ZERO):
-            if i >= arrived and c <= b % windows + (windows if b == windows else 0):
-                halo_copies[i].wait()
-                arrived += 1
-                for w in range(c, e):
-                    wide_d[w * hs : (w + 1) * hs] = hrecv[w].astype(f32)
-                    for r in top:
-                        x = w * hs + r * WIN
-                        y = (r + hw) * stride + w * WIN
-                        field_b[y : y + WIN] = wide_d[x : x + WIN]
-                if c == 0:
-                    wrap_ends(field_b, bottom)
-        if arrived == len(halo_copies):
-            cot_copy = remote(cot_in.at[pl.ds(0, hw)], grecv, 1, (gi, prev))
-            cot_copy.start()
-        to_shifted(field_b, wide_c, range(a, b), bottom)
-        rows = slice(a * SLOTS, b * SLOTS)
-        xt[1, rows] = wide_c[rows].astype(bf16)
-        layer_forward(1, a, b, wide_e)
+
+    halo_copy.wait()
+    cot_copy = remote(cot_in.at[pl.ds(0, hw)], grecv, 2, (gi, prev))
+    cot_copy.start()
+    for w in every:
+        wide_d[w * hs : (w + 1) * hs] = hrecv[w].astype(f32)
+        for r in top:
+            x = w * hs + r * WIN
+            y = (r + hw) * stride + w * WIN
+            field_b[y : y + WIN] = wide_d[x : x + WIN]
+    wrap_ends(field_b, bottom)
+    to_shifted(field_b, wide_c, bottom)
+    xt[1] = wide_c[...].astype(bf16)
+    project(1)
+    attend(1, BOTH)
+    feed_forward(1, BOTH, wide_e)
 
     for w in every:
         osend[w] = wide_e[w * SLOTS + hs : (w + 1) * SLOTS].astype(bf16)
-    out_copy = remote(osend, orecv, 2, (gi, nxt))
+    out_copy = remote(osend, orecv, 3, (gi, nxt))
     out_copy.start()
 
     cot_copy.wait()
     for r in top:
         field_c[(r + hw) * stride : (r + hw) * stride + cols] = grecv[r].astype(f32)
     wrap_ends(field_c, bottom)
-    to_shifted(field_c, wide_f, every, bottom)
-    parts = []
-    back_copies = []
-    for i, (a, b) in enumerate(BACKWARD_ONE):
-        parts.append(dense_backward(1, a, b, wide_f))
-        attention_backward(1, range(a, b))
-        input_gradient(1, a, b, wide_g)
-        for w in range(a, b):
-            bsend[w] = wide_g[w * SLOTS + hs : (w + 1) * SLOTS].astype(bf16)
-        back_copies.append(remote(bsend.at[a:b], brecv.at[a:b], 6 + i, (gi, nxt)))
-        back_copies[-1].start()
-        from_shifted(wide_g, SLOTS, field_d, hw, range(a, b))
-    wrap_starts(field_d, bottom)
-    norm_grads(1, parts)
+    to_shifted(field_c, wide_f, bottom)
+    norm_parts = [dense_backward(1, BOTH, wide_f)]
+    attention_backward(1, BOTH)
+    input_gradient(1, wide_g)
+    for w in every:
+        bsend[w] = wide_g[w * SLOTS + hs : (w + 1) * SLOTS].astype(bf16)
+    back_copy = remote(bsend, brecv, 4, (gi, nxt))
+    back_copy.start()
+
+    norm_grads(1, norm_parts)
     feed_forward_grads(1)
     attention_grads(1)
     totals[0].to_sibling()
-
-    parts = []
-    arrived = 0
-    for i, ranges in enumerate(BACKWARD_ZERO):
-        for j, (c, e) in enumerate(BACKWARD_ONE):
-            if j >= arrived and (i == len(BACKWARD_ZERO) - 1 or c < ranges[0][1]):
-                back_copies[j].wait()
-                arrived += 1
-                for w in range(c, e):
-                    wide_d[w * hs : (w + 1) * hs] = brecv[w].astype(f32)
-                from_shifted(wide_d, hs, field_d, 0, range(c, e))
-                if e == windows:
-                    wrap_starts(field_d, top)
-        if i == 0:
-            totals[0].to_chips()
-        for a, b in ranges:
-            to_windows(field_d, wide_h, range(a, b))
-            rows = slice(a * SLOTS, b * SLOTS)
-            wide_h[rows] = wide_h[rows].astype(bf16).astype(f32)
-            parts.append(dense_backward(0, a, b, wide_h))
-        if i == len(BACKWARD_ZERO) - 1:
-            feed_forward_grads(0)
-            totals[1].to_sibling()
-        attention_backward(0, [w for a, b in ranges for w in range(a, b)])
-    norm_grads(0, parts)
+    from_shifted(wide_g, SLOTS, field_d, hw)
+    wrap_starts(field_d, bottom)
+    to_windows(field_d, wide_h, bottom)
+    for w in every:
+        late = slice(w * SLOTS + hs, (w + 1) * SLOTS)
+        wide_h[late] = wide_h[late].astype(bf16).astype(f32)
+    norm_parts = [dense_backward(0, (1,), wide_h)]
+    attention_backward(0, (1,), keep=(kept_v, kept_k))
+
+    back_copy.wait()
+    totals[0].to_chips()
+    for w in every:
+        wide_d[w * hs : (w + 1) * hs] = brecv[w].astype(f32)
+    from_shifted(wide_d, hs, field_d, 0)
+    wrap_starts(field_d, top)
+    to_windows(field_d, wide_h, top)
+    norm_parts.append(dense_backward(0, (0,), wide_h))
+    feed_forward_grads(0)
+    totals[1].to_sibling()
+    attention_backward(0, (0,), add_to=(kept_v, kept_k))
+    norm_grads(0, norm_parts)
     attention_grads(0)
     totals[2].to_sibling()
-    totals[0].spread()
+    totals[1].to_chips()
     totals[2].to_chips()
-    totals[1].to_chips()
-    input_gradient(0, 0, windows, wide_a)
+    input_gradient(0, wide_a)
     for w in every:
         for r in range(WIN):
             a = w * SLOTS + r * WIN
@@ -641,16 +678,17 @@
     out_copy.wait()
     for w in every:
         wide_d[w * hs : (w + 1) * hs] = orecv[w].astype(f32)
-    from_shifted(wide_d, hs, field_c, 0, every)
-    from_shifted(wide_e, SLOTS, field_c, hw, every)
+    from_shifted(wide_d, hs, field_c, 0)
+    from_shifted(wide_e, SLOTS, field_c, hw)
     wrap_starts(field_c, range(WIN))
     for r in range(WIN):
         block_v[r] = field_c[r * stride : r * stride + cols].astype(bf16)
+    totals[0].spread()
+    totals[1].spread()
     totals[2].spread()
-    totals[1].spread()
     totals[0].share()
+    totals[1].share()
     totals[2].share()
-    totals[1].share()
     for load in state_loads:
         load.wait()
     for total in totals:
@@ -689,7 +727,7 @@
         vm((2, T, D), f32),
         vm((128, LANES), f32),
         *[vm((WIN * (cols + 8), D), f32) for _ in range(4)],
-        *[vm((T, D), f32) for _ in range(8)],
+        *[vm((T, D), f32) for _ in range(10)],
         vm((windows, SLOTS, LANES), f32),
         vm((T, D), bf16),
         vm((T, FF), bf16),

time: 47.8 us -> 44.9 us (0.939)
  Pallas kernels: 46.8 us -> 43.9 us
    pallas_call x1, Pallas kernels: 42.8 us -> 39.9 us  [body(): found = call(*held)]
where the time goes in v4:
time: 44.9 us; the launch traced here: 44.7 us
  Pallas kernels  43.9 us (98%)
  between operations  0.84 us (2%)
    pallas_call x1, Pallas kernels, body(): found = call(*held)  39.9 us
    pallas_call x1, Pallas kernels, lamb_call(): pl.pallas_call(lamb_kernel, out_shape=out, in_specs=[whole] * 23, out_spe...  3.94 us

profile of v4, /device:TPU:0, one launch (start us, length us, event | category | flops | bytes accessed | tf_op | source)
XLA Modules:
  0.0 44.7 jit_solution(15401753645285330224)
XLA Ops:
  0.7 39.9 %shard_map.372 = (bf16[12,72,128]{2,1,0:T(8,128)(2,1)S(1)}, f32[12,72,128]{2,1,0:T(8,128)S(1)}, bf16[2,16,40,128]{3,2,1,0:T(8,128)(2,1)S(1)}, bf16[2,16,16,128]{...) custom-call(bf16[12,72,128]{2,1,0:T(8,128)(2,1)} %bitcast.7, ...), custom_call_target="tpu_custom_call" | custom-call | tf_op jit(solution)/shard_map/pallas_call | solution.py:901
  40.6 3.9 %shard_map.373 = (bf16[12,72,128]{2,1,0:T(8,128)(2,1)}, f32[12,72,128]{2,1,0:T(8,128)}, f32[2,128,384]{2,1,0:T(8,128)}, f32[2,128,128]{2,1,0:T(8,128)}, f32[2,12...) custom-call(bf16[2,16,40,128]{3,2,1,0:T(8,128)(2,1)S(1)} %get-tuple-, ...), custom_call_target="tpu_custom_call" | custom-call | tf_op jit(solution)/shard_map/pallas_call | solution.py:883

commit v5 on v4

--- a/solution.py
+++ b/solution.py
@@ -27,10 +27,9 @@
 epsilon = 1e-06
 clip_bound = 1.0
 
-L1 = dict(q=0, k=128, v=256, o=384, e=512, r=768, p=1024, n=1168)
-L0_FF = dict(e=0, r=256)
-L0_REST = dict(q=0, k=128, v=256, o=384, p=512, n=656)
-SET_ROWS = (1176, 512, 664)
+FEED = dict(e=0, r=256)
+REST = dict(q=0, k=128, v=256, o=384, p=512, n=656)
+SET_ROWS = (664, 512, 664, 512)
 
 PARTS = ((0, 80), (80, SLOTS))
 BOTH = (0, 1)
@@ -94,7 +93,7 @@
     *refs,
 ):
     states_in, refs = refs[:12], refs[12:]
-    outs, refs = refs[:23], refs[23:]
+    outs, refs = refs[:24], refs[24:]
     run(strips, windows, n_grid, feat_in, codes_in, cot_in, attend_in, output_in, expand_in,
         reduce_in, position_in, norms_in, states_in, outs, *refs)
 
@@ -197,7 +196,7 @@
                 others.append((g_p * n_z + z_p, (g_p, z_p * 2 + core)))
 
     block_v, input_v = outs[0:2]
-    attend_w, output_w, expand_w, reduce_w, position, norms = outs[5:11]
+    attend_w, output_w, expand_w, reduce_w, position, norms = outs[6:12]
     loads = {}
     for i, (src, dst) in enumerate(
         (
@@ -216,7 +215,7 @@
         loads[i].start()
 
     state_loads = []
-    for i, (src, dst) in enumerate(zip(states_in, outs[11:23])):
+    for i, (src, dst) in enumerate(zip(states_in, outs[12:24])):
         state_loads.append(pltpu.make_async_copy(src, dst, out_sem.at[i]))
 
     barrier = pltpu.get_barrier_semaphore()
@@ -287,15 +286,10 @@
         def done(self):
             self.last.wait()
 
-    totals = [Total(n) for n in range(3)]
+    totals = [Total(n) for n in range(4)]
     number_of = totals.index
-    homes = (
-        {"e": (totals[1], L0_FF), "r": (totals[1], L0_FF)},
-        {},
-    )
-
     def put(l, name, value, rows):
-        total, table = homes[l].get(name, (totals[2], L0_REST) if l == 0 else (totals[0], L1))
+        total, table = (totals[3 if l else 1], FEED) if name in FEED else (totals[0 if l else 2], REST)
         total.g[table[name] : table[name] + rows] = value
 
     def code_tables(l, table):
@@ -632,6 +626,8 @@
     wrap_ends(field_c, bottom)
     to_shifted(field_c, wide_f, bottom)
     norm_parts = [dense_backward(1, BOTH, wide_f)]
+    feed_forward_grads(1)
+    totals[3].to_sibling()
     attention_backward(1, BOTH)
     input_gradient(1, wide_g)
     for w in every:
@@ -639,8 +635,8 @@
     back_copy = remote(bsend, brecv, 4, (gi, nxt))
     back_copy.start()
 
+    totals[3].to_chips()
     norm_grads(1, norm_parts)
-    feed_forward_grads(1)
     attention_grads(1)
     totals[0].to_sibling()
     from_shifted(wide_g, SLOTS, field_d, hw)
@@ -662,6 +658,7 @@
     norm_parts.append(dense_backward(0, (0,), wide_h))
     feed_forward_grads(0)
     totals[1].to_sibling()
+    totals[3].spread()
     attention_backward(0, (0,), add_to=(kept_v, kept_k))
     norm_grads(0, norm_parts)
     attention_grads(0)
@@ -686,6 +683,7 @@
     totals[0].spread()
     totals[1].spread()
     totals[2].spread()
+    totals[3].share()
     totals[0].share()
     totals[1].share()
     totals[2].share()
@@ -759,7 +757,7 @@
             vm((chips, c, D), bf16),
         ]
         outs.append(vm((2, chips, c, D), bf16))
-    copies = COPIES + 3 * 4
+    copies = COPIES + 4 * 4
     scratch += [pltpu.SemaphoreType.DMA((n,)) for n in (copies, copies, 9, 12)]
     params = [(2, D, 3 * D), (2, D, D), (2, D, FF), (2, FF, D), (2, SLOTS, D), (2, 4, D)]
     outs += [vm(shape, f32) for shape in params * 3]
@@ -773,7 +771,7 @@
             *outs,
         ),
         in_specs=[far] * 21,
-        out_specs=(near,) * 23,
+        out_specs=(near,) * 24,
         scratch_shapes=scratch,
         compiler_params=pltpu.CompilerParams(
             collective_id=0, has_side_effects=True, vmem_limit_bytes=40 * 1024 * 1024
@@ -782,14 +780,14 @@
 
 
 def lamb_kernel(*refs):
-    grads_near = refs[0:3]
-    block_near, input_near = refs[3:5]
-    states = refs[5:23]
-    block_out, input_out = refs[23:25]
-    results_far = refs[25:43]
-    clip_out, norms_out = refs[43:45]
-    results = refs[45:63]
-    out_sem, cell_sem = refs[63:65]
+    grads_near = refs[0:4]
+    block_near, input_near = refs[4:6]
+    states = refs[6:24]
+    block_out, input_out = refs[24:26]
+    results_far = refs[26:44]
+    clip_out, norms_out = refs[44:46]
+    results = refs[46:64]
+    out_sem, cell_sem = refs[64:66]
     cells = [
         pltpu.make_async_copy(block_near, block_out, cell_sem.at[0]),
         pltpu.make_async_copy(input_near, input_out, cell_sem.at[1]),
@@ -807,12 +805,10 @@
     fix_two = 1.0 / (1.0 - beta_two**STEP)
 
     def grad_rows(l, name, start, rows):
-        if l == 1:
-            number, table = 0, L1
-        elif name in L0_FF:
-            number, table = 1, L0_FF
+        if name in FEED:
+            number, table = (3 if l else 1), FEED
         else:
-            number, table = 2, L0_REST
+            number, table = (0 if l else 2), REST
         return grads[number][table[name] + start : table[name] + start + rows]
 
     def step(index, where, grad, decay):
@@ -883,7 +879,7 @@
     return pl.pallas_call(
         lamb_kernel,
         out_shape=out,
-        in_specs=[whole] * 23,
+        in_specs=[whole] * 24,
         out_specs=[far] * 20 + [whole] * 2,
         scratch_shapes=near + [pltpu.SemaphoreType.DMA((n,)) for n in (18, 2)],
         compiler_params=pltpu.CompilerParams(vmem_limit_bytes=32 * 1024 * 1024),
@@ -899,7 +895,7 @@
         for a in (features[0], cell_frame, cotangent[0], *rest)
     ]
     found = call(*held)
-    out = lamb_call(found[2:5], found[0], found[1], found[5:23])
+    out = lamb_call(found[2:6], found[0], found[1], found[6:24])
     norms = jnp.swapaxes(out[21], 1, 2)
     return (out[0][None], out[1][None], *out[2:20], out[20].reshape(()), norms)
 

time: 44.9 us -> 44.7 us (level)
  no operation moved by 1% of the time
where the time goes in v5:
time: 44.7 us; the launch traced here: 44.6 us
  Pallas kernels  43.7 us (98%)
  between operations  0.84 us (2%)
    pallas_call x1, Pallas kernels, body(): found = call(*held)  39.8 us
    pallas_call x1, Pallas kernels, lamb_call(): pl.pallas_call(lamb_kernel, out_shape=out, in_specs=[whole] * 24, out_spe...  3.88 us

profile of v5, /device:TPU:0, one launch (start us, length us, event | category | flops | bytes accessed | tf_op | source)
XLA Modules:
  0.0 44.6 jit_solution(1515108472221714792)
XLA Ops:
  0.7 39.8 %shard_map.372 = (bf16[12,72,128]{2,1,0:T(8,128)(2,1)S(1)}, f32[12,72,128]{2,1,0:T(8,128)S(1)}, bf16[2,16,24,128]{3,2,1,0:T(8,128)(2,1)S(1)}, bf16[2,16,16,128]{...) custom-call(bf16[12,72,128]{2,1,0:T(8,128)(2,1)} %bitcast.7, ...), custom_call_target="tpu_custom_call" | custom-call | tf_op jit(solution)/shard_map/pallas_call | solution.py:897
  40.5 3.9 %shard_map.373 = (bf16[12,72,128]{2,1,0:T(8,128)(2,1)}, f32[12,72,128]{2,1,0:T(8,128)}, f32[2,128,384]{2,1,0:T(8,128)}, f32[2,128,128]{2,1,0:T(8,128)}, f32[2,12...) custom-call(bf16[2,16,24,128]{3,2,1,0:T(8,128)(2,1)S(1)} %get-tuple-, ...), custom_call_target="tpu_custom_call" | custom-call | tf_op jit(solution)/shard_map/pallas_call | solution.py:879
